TPU v7x, 512 devices: a whole 4x4x16 slice. The times are simulated.
512 devices in a mesh: dp: 32 (over z, core), tensor: 16 (over y, x).
Axes of the slice: x: 4, y: 4, z: 16, core: 2. Of those that a mesh axis runs over, the one named last changes fastest.
Arguments:
- hidden: bfloat16 [4096, 18432], P('dp', 'tensor'), may hold values from -66 to 66
- grad_out: bfloat16 [4096, 4608], P('dp'), may hold values from -192 to 192
- seg_ids: int32 [4096], replicated, may hold values from 0 to 7, as said below
- seg_counts: int32 [256], P('dp'), may hold values from 1 to 31, as said below
- added_noise: bfloat16 [4608, 18432], P('dp', 'tensor'), may hold values from -6 to 6
Outputs:
- weight_grad: bfloat16 [4608, 18432], P('dp', 'tensor')
- example_norms: float32 [256], P('dp')
Inputs may be any that keep to these rules, and one draw needn't show every extreme that they name: `seg_ids`: within each sequence the ids never fall and every one of the 8 ids occurs. seg_counts[j * 8 + i] is the number of tokens of sequence j whose id is i; the counts of a sequence sum to 128.
All inputs are finite; a program needn't handle non-finite values.
Results may differ from a plain program's by a relative error of at most 0.012.
Values may be sent and summed in bfloat16 or wider, within the bound.
No kernel may reach another device: no remote copies, remote signals or barrier semaphores. Data moves between devices by JAX's collectives and lax.ppermute only.
A program may use at most 64 MiB of HBM per device.

v0:
```python
import jax
import jax.numpy as jnp
from jax import lax
from jax.sharding import PartitionSpec as P

D = 4608
FFW = 18432
SEQ = 128
NSEG = 8


EPSILON = 1e-06
CLIP_FRACTION = 4.2


def clip_bound():
    return CLIP_FRACTION * (FFW * D * NSEG / SEQ) ** 0.5


def per_device(hidden, grad_out, seg_ids, seg_counts, added_noise):
    seq_len = hidden.shape[0]
    seg_total = seg_counts.shape[0]
    group_index = lax.axis_index("dp")
    own_segments = lax.dynamic_slice_in_dim(seg_ids, group_index * seq_len, seq_len)
    member = (own_segments[:, None] == jnp.arange(seg_total, dtype=jnp.int32)[None, :]).astype(
        jnp.float32
    )
    tok_count = jnp.dot(member, seg_counts.astype(jnp.float32), precision=lax.Precision.HIGHEST)
    scaled_local = (grad_out.astype(jnp.float32) / tok_count[:, None]).astype(jnp.bfloat16)
    gram_scaled = lax.dot_general(
        scaled_local, scaled_local, (((1,), (1,)), ((), ())), preferred_element_type=jnp.float32
    )
    gram_hidden = lax.dot_general(
        hidden, hidden, (((1,), (1,)), ((), ())), preferred_element_type=jnp.float32
    )
    partial_sq = jnp.sum(
        member * jnp.dot(gram_hidden * gram_scaled, member, precision=lax.Precision.HIGHEST), axis=0
    )
    group_sq = lax.psum(partial_sq, "tensor")
    own_norm = jnp.sqrt(group_sq + EPSILON)
    own_factor = jnp.minimum(1.0, clip_bound() / own_norm)
    tok_factor = jnp.dot(member, own_factor, precision=lax.Precision.HIGHEST)
    weighted_rows = (scaled_local.astype(jnp.float32) * tok_factor[:, None]).astype(jnp.bfloat16)
    weighted = lax.all_to_all(weighted_rows, "dp", split_axis=1, concat_axis=0, tiled=True)
    summed = lax.dot_general(
        weighted,
        lax.all_gather(hidden, "dp", axis=0, tiled=True),
        (((0,), (0,)), ((), ())),
        preferred_element_type=jnp.float32,
    )
    weight_grad = (summed + added_noise.astype(jnp.float32)).astype(jnp.bfloat16)
    return (weight_grad, own_norm)


def solution(mesh):
    placed = (P("dp", "tensor"), P("dp", None), P(), P("dp"), P("dp", "tensor"))
    return jax.shard_map(
        per_device,
        mesh=mesh,
        in_specs=placed,
        out_specs=(P("dp", "tensor"), P("dp")),
        check_vma=False,
    )
```

profile of v0, /device:TPU:1, one launch (start us, length us, event | category | flops | bytes accessed | tf_op | source)
XLA Modules:
  0.0 156.6 jit_solution(6809469331345152475)
XLA Ops:
  7.2 0.0 all-gather.2.cloned.1.call-start
  7.2 0.7 all-gather.2.cloned.1.call-update
  7.9 0.0 copy-start.2
  7.9 0.0 copy-start
  7.9 1.7 %copy.7 = bf16[128,4608]{0,1:T(8,128)(2,1)S(1)} copy(bf16[128,4608]{1,0:T(8,128)(2,1)} %param.6) | data formatting | bytes 2359296 | tf_op args[1]
  9.7 0.8 dynamic_slice.3
  10.4 0.0 copy-done.2
  10.4 0.1 convolution_bitcast_fusion.1
  10.6 0.0 copy-done
  10.6 0.2 fusion.12
  10.8 0.5 convolution_multiply_fusion
  11.4 0.3 fusion.3
  11.7 34.3 %psum.7 = f32[8]{0:T(128)S(1)} all-reduce(f32[8]{0:T(128)S(1)} %fusion.3), channel_id=1, replica_groups=mesh['dp'=32,'tensor'=16] {'tensor'}, use_global_device_ids=true, to_apply=%region_1.0 | all-reduce | flops 8 | bytes 64 | tf_op jit(solution)/shard_map/psum | solution.py:39
  45.9 0.0 copy-start.3
  45.9 0.1 convolution_bitcast_fusion
  46.0 0.3 multiply_convert_fusion
  46.4 0.1 copy-done.3
  46.4 0.0 copy-start.1
  46.4 96.1 %all_to_all.19 = bf16[128,32,144]{0,2,1:T(8,128)(2,1)S(1)} all-to-all(bf16[128,32,144]{0,2,1:T(8,128)(2,1)S(1)} %bitcast.23), channel_id=1, replica_groups=mesh['dp'=32,'tensor'=16] {'dp'}, dimensions={1} | all-to-all | bytes 2359296 | tf_op jit(solution)/shard_map/all_to_all | solution.py:44
  142.5 1.1 all-gather.2.cloned.1.call-done
  143.6 0.0 copy-done.1
  143.6 6.1 %fusion = bf16[144,1152]{1,0:T(8,128)(2,1)} fusion(bf16[4096,1152]{1,0:T(8,128)(2,1)} %all-gather.2.cloned.1.call-done, bf16[144,1152]{1,0:T(8,128)(2,1)S(1)} %copy-done.1, bf16[128,32,144]{0,2,1:T(8,128)(2,1)S(1)} %all_to_all.19), kind=kOutput, calls=%fused_computation.1 | convolution fusion | flops 1359452160 | bytes 11280384 | tf_op jit(solution)/shard_map/dot_general | solution.py:45
  (1 shorter events, 0.0 us)
Async XLA Ops:
  7.2 136.5 %all-gather.2.cloned.1.call-start = ((), (), s32[]{:S(2)}) async-start(), calls=%async_computation.1 | async-start | bytes 9732096 | tf_op jit(solution)/shard_map/all_gather | solution.py:47
  7.9 2.5 %copy-start.2 = (s32[8]{0:T(128)S(1)}, s32[8]{0:T(128)}, u32[]{:S(2)}) copy-start(s32[8]{0:T(128)} %param.8) | copy-start | bytes 100
  7.9 2.6 %copy-start = (bf16[128,1152]{1,0:T(8,128)(2,1)S(1)}, bf16[128,1152]{1,0:T(8,128)(2,1)}, u32[]{:S(2)}) copy-start(bf16[128,1152]{1,0:T(8,128)(2,1)} %param.5) | copy-start | bytes 884740
  45.9 0.5 copy-start.3
  46.4 97.2 %copy-start.1 = (bf16[144,1152]{1,0:T(8,128)(2,1)S(1)}, bf16[144,1152]{1,0:T(8,128)(2,1)}, u32[]{:S(2)}) copy-start(bf16[144,1152]{1,0:T(8,128)(2,1)} %param.9) | copy-start | bytes 995332
Sparse Core Ops, SparseCore 0:
  10.1 133.4 all-gather.1
where the time goes:
time: 157 us
  blocking collectives  130 us (83%)
  between operations  14.1 us (9%)
  matrix products  7.43 us (5%)
  local copies, waits for them, and re-layouts  2.58 us (2%)
  waiting for transfers between devices  1.77 us (1%)
    all_to_all x1, blocking collectives, per_device(): lax.all_to_all(weighted_rows, 'dp', split_axis=1, concat_axis=0, tiled=True)  96.1 us
    psum x1, blocking collectives, per_device(): group_sq = lax.psum(partial_sq, 'tensor')  34.3 us
    dot_general x1, matrix products, per_device(): lax.dot_general(weighted, lax.all_gather(hidden, 'dp', axis=0, tiled=True...  6.11 us
  transfers between devices with their start and end apart: 1, of which 1 were waited for; matrix products, arithmetic and copies ran while one was open for 3% of the time, Pallas kernels for 0%

commit v1 on v0

v1 whole, which is shorter than its diff:
```python
import jax
import jax.numpy as jnp
from jax import lax
from jax.experimental import pallas as pl
from jax.experimental.pallas import tpu as pltpu
from jax.sharding import PartitionSpec as P

D = 4608
FFW = 18432
SEQ = 128
NSEG = 8
PLANES = 16
ROW = 4
ROWS = 144

EPSILON = 1e-06
CLIP_FRACTION = 4.2


def clip_bound():
    return CLIP_FRACTION * (FFW * D * NSEG / SEQ) ** 0.5


def mix(value, stride):
    return [
        lax.ppermute(value, "tensor", [(i, i ^ (k * stride)) for i in range(ROW * ROW)])
        for k in range(1, ROW)
    ]


def plane_sum(value):
    for stride in (1, ROW):
        one, two, three = mix(value, stride)
        value = (value + one) + (two + three)
    return value


def plane_gather(value):
    for stride in (1, ROW):
        value = jnp.concatenate([value] + mix(value, stride), axis=0)
    return value


def shift_perm(cross):
    perm = []
    for plane in range(PLANES):
        for core in range(2):
            for j in range(ROW * ROW):
                to = ((plane + j) % PLANES) * 2 + (1 - core if cross else core)
                perm.append(((plane * 2 + core) * 16 + j, to * 16 + j))
    return perm


def product_kernel(place, w_ref, h_ref, noise_ref, out_ref, acc_ref):
    step = pl.program_id(0)

    @pl.when(step == 0)
    def _():
        acc_ref[...] = jnp.zeros_like(acc_ref)

    acc_ref[...] += jnp.dot(w_ref[0], h_ref[0], preferred_element_type=jnp.float32)

    @pl.when(step == pl.num_programs(0) - 1)
    def _():
        out_ref[...] = (acc_ref[...] + noise_ref[...].astype(jnp.float32)).astype(jnp.bfloat16)


def product(place, w_all, h_all, noise):
    columns = h_all.shape[-1]
    return pl.pallas_call(
        product_kernel,
        grid_spec=pltpu.PrefetchScalarGridSpec(
            num_scalar_prefetch=1,
            grid=(PLANES,),
            in_specs=[
                pl.BlockSpec((1, ROWS, 256), lambda s, p: (((p[0] + PLANES - s) % PLANES) ^ p[1], 0, 0)),
                pl.BlockSpec((1, 256, columns), lambda s, p: (s, 0, 0)),
                pl.BlockSpec((ROWS, columns), lambda s, p: (0, 0)),
            ],
            out_specs=pl.BlockSpec((ROWS, columns), lambda s, p: (0, 0)),
            scratch_shapes=[pltpu.VMEM((ROWS, columns), jnp.float32)],
        ),
        out_shape=jax.ShapeDtypeStruct((ROWS, columns), jnp.bfloat16),
        compiler_params=pltpu.CompilerParams(vmem_limit_bytes=24 * 1024 * 1024),
        cost_estimate=pl.CostEstimate(
            flops=2 * 4096 * ROWS * columns, bytes_accessed=2 * 4096 * (ROWS + columns), transcendentals=0
        ),
    )(place, w_all, h_all, noise)


def per_device(hidden, grad_out, seg_ids, seg_counts, added_noise):
    dp = lax.axis_index("dp")
    j = lax.axis_index("tensor")
    plane, core = dp // 2, dp % 2
    h_all = lax.all_gather(hidden, "dp", axis=0, tiled=True)

    own = lax.dynamic_slice_in_dim(seg_ids, dp * SEQ, SEQ)
    member = own[:, None] == jnp.arange(NSEG, dtype=jnp.int32)[None, :]
    same = own[:, None] == own[None, :]

    def per_token(values):
        return jnp.sum(jnp.where(member, values[None, :], 0.0), axis=1)

    tok_count = per_token(seg_counts.astype(jnp.float32))
    scaled = (grad_out.astype(jnp.float32) / tok_count[:, None]).astype(jnp.bfloat16)
    contract = (((1,), (1,)), ((), ()))
    gram_scaled = lax.dot_general(scaled, scaled, contract, preferred_element_type=jnp.float32)
    gram_hidden = lax.dot_general(hidden, hidden, contract, preferred_element_type=jnp.float32)
    rows = jnp.sum(jnp.where(same, gram_hidden * gram_scaled, 0.0), axis=1)
    partial_sq = jnp.sum(jnp.where(member, rows[:, None], 0.0), axis=0)
    own_norm = jnp.sqrt(plane_sum(partial_sq) + EPSILON)
    tok_factor = per_token(jnp.minimum(1.0, clip_bound() / own_norm))

    target = (plane + j) % PLANES
    piece = lax.dynamic_slice_in_dim(scaled, target * (2 * ROWS), 2 * ROWS, 1)
    piece = (piece.astype(jnp.float32) * tok_factor[:, None]).astype(jnp.bfloat16).T
    first = core == 0
    keep = lax.ppermute(jnp.where(first, piece[:ROWS], piece[ROWS:]), ("dp", "tensor"), shift_perm(False))
    swap = lax.ppermute(jnp.where(first, piece[ROWS:], piece[:ROWS]), ("dp", "tensor"), shift_perm(True))
    block = jnp.concatenate([jnp.where(first, keep, swap), jnp.where(first, swap, keep)], axis=1)
    w_all = plane_gather(block[None])

    place = jnp.stack([plane, j]).astype(jnp.int32)
    weight_grad = product(place, w_all, h_all.reshape(PLANES, 2 * SEQ, -1), added_noise)
    return (weight_grad, own_norm)


def solution(mesh):
    placed = (P("dp", "tensor"), P("dp", None), P(), P("dp"), P("dp", "tensor"))
    return jax.shard_map(
        per_device,
        mesh=mesh,
        in_specs=placed,
        out_specs=(P("dp", "tensor"), P("dp")),
        check_vma=False,
    )
```

time: 157 us -> 123 us (0.78)
  the two profiles are of different devices: /device:TPU:1 before, /device:TPU:15 now
where the time goes in v1:
time: 123 us; the launch traced here: 122 us
  starting transfers between devices  62.1 us (50%)
  waiting for transfers between devices  31.1 us (25%)
  between operations  14.3 us (12%)
  local copies, waits for them, and re-layouts  6.27 us (5%)
  Pallas kernels  6.04 us (5%)
  other arithmetic  1.89 us (2%)
    ppermute x12, starting transfers between devices, mix(): lax.ppermute(value, 'tensor', [(i, i ^ k * stride) for i in range(ROW * R...  37.8 us
    ppermute x12, waiting for transfers between devices, mix(): lax.ppermute(value, 'tensor', [(i, i ^ k * stride) for i in range(ROW * R...  15.8 us
    ppermute x1, starting transfers between devices, per_device(): lax.ppermute(jnp.where(first, piece[:ROWS], piece[ROWS:]), ('dp', 'tensor...  12.9 us
    ppermute x1, starting transfers between devices, per_device(): lax.ppermute(jnp.where(first, piece[ROWS:], piece[:ROWS]), ('dp', 'tensor...  11.3 us
    all_gather x1, waiting for transfers between devices, per_device(): h_all = lax.all_gather(hidden, 'dp', axis=0, tiled=True)  8.74 us
    pallas_call x1, Pallas kernels, product(): pl.pallas_call(product_kernel, grid_spec=pltpu.PrefetchScalarGridSpec(num...  6.04 us
    ppermute x1, waiting for transfers between devices, per_device(): lax.ppermute(jnp.where(first, piece[ROWS:], piece[:ROWS]), ('dp', 'tensor...  5.82 us
    unnamed x12, local copies, waits for them, and re-layouts  5.49 us
  transfers between devices with their start and end apart: 15, of which 7 were waited for; matrix products, arithmetic and copies ran while one was open for 4% of the time, Pallas kernels for 0%

profile of v1, /device:TPU:15, one launch (start us, length us, event | category | flops | bytes accessed | tf_op | source)
XLA Modules:
  0.0 122.5 jit_solution(8780877289432678147)
XLA Ops:
  7.2 0.7 all-gather.2.cloned.1.call-update
  7.9 0.7 convert_element_type.16
  8.6 1.7 %copy.8 = bf16[128,4608]{0,1:T(8,128)(2,1)S(1)} copy(bf16[128,4608]{1,0:T(8,128)(2,1)} %param.6) | data formatting | bytes 2359296 | tf_op args[1]
  10.3 0.8 dynamic_slice.6
  11.2 0.2 fusion.3
  11.4 0.2 divide_convert_fusion
  11.6 0.5 fusion.1
  12.2 0.1 select_reduce_fusion.1
  12.3 2.5 %collective-permute-start = (f32[8]{0:T(128)S(1)}, f32[8]{0:T(128)S(1)}, u32[]{:S(2)}, u32[]{:S(2)}) collective-permute-start(f32[8]{0:T(128)S(1)} %select_reduce_fusion.1), channel_id=1, source_target_pairs={{0,1},{1,0},{2,3},{3,2},{4,5},{5,4},{6,7},{7,6},{8,9},{9,8},{10,11... | collective-permute-start | bytes 104 | tf_op jit(solution)/shard_map/ppermute | solution.py:26
  14.8 2.7 %collective-permute-start.1 = (f32[8]{0:T(128)S(1)}, f32[8]{0:T(128)S(1)}, u32[]{:S(2)}, u32[]{:S(2)}) collective-permute-start(f32[8]{0:T(128)S(1)} %select_reduce_fusion.1), channel_id=1, source_target_pairs={{0,2},{1,3},{2,0},{3,1},{4,6},{5,7},{6,4},{7,5},{8,10},{9,11},{10,... | collective-permute-start | bytes 104 | tf_op jit(solution)/shard_map/ppermute | solution.py:26
  17.5 4.4 %collective-permute-start.2 = (f32[8]{0:T(128)S(1)}, f32[8]{0:T(128)S(1)}, u32[]{:S(2)}, u32[]{:S(2)}) collective-permute-start(f32[8]{0:T(128)S(1)} %select_reduce_fusion.1), channel_id=1, source_target_pairs={{0,3},{1,2},{2,1},{3,0},{4,7},{5,6},{6,5},{7,4},{8,11},{9,10},{10,... | collective-permute-start | bytes 104 | tf_op jit(solution)/shard_map/ppermute | solution.py:26
  22.0 1.0 collective-permute-done.2
  23.0 1.9 %collective-permute-start.3 = (f32[8]{0:T(128)S(1)}, f32[8]{0:T(128)S(1)}, u32[]{:S(2)}, u32[]{:S(2)}) collective-permute-start(f32[8]{0:T(128)S(1)} %add_add_fusion), channel_id=1, source_target_pairs={{0,4},{1,5},{2,6},{3,7},{4,0},{5,1},{6,2},{7,3},{8,12},{9,13},{10,... | collective-permute-start | bytes 104 | tf_op jit(solution)/shard_map/ppermute | solution.py:26
  24.9 4.4 %collective-permute-start.4 = (f32[8]{0:T(128)S(1)}, f32[8]{0:T(128)S(1)}, u32[]{:S(2)}, u32[]{:S(2)}) collective-permute-start(f32[8]{0:T(128)S(1)} %add_add_fusion), channel_id=1, source_target_pairs={{0,8},{1,9},{2,10},{3,11},{4,12},{5,13},{6,14},{7,15},{8,0},{9,1},... | collective-permute-start | bytes 104 | tf_op jit(solution)/shard_map/ppermute | solution.py:26
  29.3 2.1 %collective-permute-start.5 = (f32[8]{0:T(128)S(1)}, f32[8]{0:T(128)S(1)}, u32[]{:S(2)}, u32[]{:S(2)}) collective-permute-start(f32[8]{0:T(128)S(1)} %add_add_fusion), channel_id=1, source_target_pairs={{0,12},{1,13},{2,14},{3,15},{4,8},{5,9},{6,10},{7,11},{8,4},{9,5},... | collective-permute-start | bytes 104 | tf_op jit(solution)/shard_map/ppermute | solution.py:26
  31.4 2.6 %collective-permute-done.5 = f32[8]{0:T(128)S(1)} collective-permute-done((f32[8]{0:T(128)S(1)}, f32[8]{0:T(128)S(1)}, u32[]{:S(2)}, u32[]{:S(2)}) %collective-permute-start.5) | collective-permute-done | bytes 64 | tf_op jit(solution)/shard_map/ppermute | solution.py:26
  34.0 0.5 divide_minimum_fusion
  34.6 12.9 %collective-permute-start.6 = (bf16[144,128]{1,0:T(8,128)(2,1)S(1)}, bf16[144,128]{1,0:T(8,128)(2,1)S(1)}, u32[]{:S(2)}, u32[]{:S(2)}) collective-permute-start(bf16[144,128]{1,0:T(8,128)(2,1)S(1)} %get-tuple-element.6), channel_id=1, source_target_pairs={{0,0},{1,33},{2,66},{3,99},{4,132},{5,165},{6,198},{7,231},{8,264}... | collective-permute-start | bytes 110600 | tf_op jit(solution)/shard_map/ppermute | solution.py:118
  47.5 11.3 %collective-permute-start.7 = (bf16[144,128]{1,0:T(8,128)(2,1)S(1)}, bf16[144,128]{1,0:T(8,128)(2,1)S(1)}, u32[]{:S(2)}, u32[]{:S(2)}) collective-permute-start(bf16[144,128]{1,0:T(8,128)(2,1)S(1)} %get-tuple-element.7), channel_id=1, source_target_pairs={{0,16},{1,49},{2,82},{3,115},{4,148},{5,181},{6,214},{7,247},{8,28... | collective-permute-start | bytes 110600 | tf_op jit(solution)/shard_map/ppermute | solution.py:119
  59.0 5.8 %collective-permute-done.7 = bf16[144,128]{1,0:T(8,128)(2,1)S(1)} collective-permute-done((bf16[144,128]{1,0:T(8,128)(2,1)S(1)}, bf16[144,128]{1,0:T(8,128)(2,1)S(1)}, u32[]{:S(2)}, u32[]{:S(2)}) %collective-permute-start.7) | collective-permute-done | bytes 36896 | tf_op jit(solution)/shard_map/ppermute | solution.py:119
  64.8 1.9 %collective-permute-start.10 = (bf16[1,144,256]{2,1,0:T(8,128)(2,1)S(1)}, bf16[1,144,256]{2,1,0:T(8,128)(2,1)S(1)}, u32[]{:S(2)}, u32[]{:S(2)}) collective-permute-start(bf16[1,144,256]{2,1,0:T(8,128)(2,1)S(1)} %maximum_bitcast_fusion), channel_id=1, source_target_pairs={{0,3},{1,2},{2,1},{3,0},{4,7},{5,6},{6,5},{7,4},{8,11},{9,10},{10,... | collective-permute-start | bytes 221192 | tf_op jit(solution)/shard_map/ppermute | solution.py:26
  66.7 1.9 %collective-permute-start.8 = (bf16[1,144,256]{2,1,0:T(8,128)(2,1)S(1)}, bf16[1,144,256]{2,1,0:T(8,128)(2,1)S(1)}, u32[]{:S(2)}, u32[]{:S(2)}) collective-permute-start(bf16[1,144,256]{2,1,0:T(8,128)(2,1)S(1)} %maximum_bitcast_fusion), channel_id=1, source_target_pairs={{0,1},{1,0},{2,3},{3,2},{4,5},{5,4},{6,7},{7,6},{8,9},{9,8},{10,11... | collective-permute-start | bytes 221192 | tf_op jit(solution)/shard_map/ppermute | solution.py:26
  68.7 5.7 %collective-permute-start.9 = (bf16[1,144,256]{2,1,0:T(8,128)(2,1)S(1)}, bf16[1,144,256]{2,1,0:T(8,128)(2,1)S(1)}, u32[]{:S(2)}, u32[]{:S(2)}) collective-permute-start(bf16[1,144,256]{2,1,0:T(8,128)(2,1)S(1)} %maximum_bitcast_fusion), channel_id=1, source_target_pairs={{0,2},{1,3},{2,0},{3,1},{4,6},{5,7},{6,4},{7,5},{8,10},{9,11},{10,... | collective-permute-start | bytes 221192 | tf_op jit(solution)/shard_map/ppermute | solution.py:26
  74.5 1.7 %collective-permute-done.9 = bf16[1,144,256]{2,1,0:T(8,128)(2,1)S(1)} collective-permute-done((bf16[1,144,256]{2,1,0:T(8,128)(2,1)S(1)}, bf16[1,144,256]{2,1,0:T(8,128)(2,1)S(1)}, u32[]{:S(2)}, u32[]{:S(2)}) %collective-permute-start.9) | collective-permute-done | bytes 73760 | tf_op jit(solution)/shard_map/ppermute | solution.py:26
  76.2 2.1 %collective-permute-start.11 = (bf16[4,144,256]{2,1,0:T(8,128)(2,1)S(1)}, bf16[4,144,256]{2,1,0:T(8,128)(2,1)S(1)}, u32[]{:S(2)}, u32[]{:S(2)}) collective-permute-start(bf16[4,144,256]{2,1,0:T(8,128)(2,1)S(1)} %pad_maximum_fusion), channel_id=1, source_target_pairs={{0,4},{1,5},{2,6},{3,7},{4,0},{5,1},{6,2},{7,3},{8,12},{9,13},{10,... | collective-permute-start | bytes 884744 | tf_op jit(solution)/shard_map/ppermute | solution.py:26
  78.3 6.3 %collective-permute-start.12 = (bf16[4,144,256]{2,1,0:T(8,128)(2,1)S(1)}, bf16[4,144,256]{2,1,0:T(8,128)(2,1)S(1)}, u32[]{:S(2)}, u32[]{:S(2)}) collective-permute-start(bf16[4,144,256]{2,1,0:T(8,128)(2,1)S(1)} %pad_maximum_fusion), channel_id=1, source_target_pairs={{0,8},{1,9},{2,10},{3,11},{4,12},{5,13},{6,14},{7,15},{8,0},{9,1},... | collective-permute-start | bytes 884744 | tf_op jit(solution)/shard_map/ppermute | solution.py:26
  84.6 1.9 %collective-permute-start.13 = (bf16[4,144,256]{2,1,0:T(8,128)(2,1)S(1)}, bf16[4,144,256]{2,1,0:T(8,128)(2,1)S(1)}, u32[]{:S(2)}, u32[]{:S(2)}) collective-permute-start(bf16[4,144,256]{2,1,0:T(8,128)(2,1)S(1)} %pad_maximum_fusion), channel_id=1, source_target_pairs={{0,12},{1,13},{2,14},{3,15},{4,8},{5,9},{6,10},{7,11},{8,4},{9,5},... | collective-permute-start | bytes 884744 | tf_op jit(solution)/shard_map/ppermute | solution.py:26
  86.6 4.9 %collective-permute-done.12 = bf16[4,144,256]{2,1,0:T(8,128)(2,1)S(1)} collective-permute-done((bf16[4,144,256]{2,1,0:T(8,128)(2,1)S(1)}, bf16[4,144,256]{2,1,0:T(8,128)(2,1)S(1)}, u32[]{:S(2)}, u32[]{:S(2)}) %collective-permute-start.12) | collective-permute-done | bytes 294944 | tf_op jit(solution)/shard_map/ppermute | solution.py:26
  91.5 5.6 %collective-permute-done.13 = bf16[4,144,256]{2,1,0:T(8,128)(2,1)S(1)} collective-permute-done((bf16[4,144,256]{2,1,0:T(8,128)(2,1)S(1)}, bf16[4,144,256]{2,1,0:T(8,128)(2,1)S(1)}, u32[]{:S(2)}, u32[]{:S(2)}) %collective-permute-start.13) | collective-permute-done | bytes 294944 | tf_op jit(solution)/shard_map/ppermute | solution.py:26
  97.2 8.7 %all-gather.2.cloned.1.call-done = bf16[4096,1152]{1,0:T(8,128)(2,1)} async-done(((bf16[128,1152]{1,0:T(8,128)(2,1)}), bf16[4096,1152]{1,0:T(8,128)(2,1)}) %all-gather.2.cloned.1.call-update) | async-done | bytes 9437200 | tf_op jit(solution)/shard_map/all_gather | solution.py:95
  105.9 3.7 %copy-done = bf16[4096,1152]{1,0:T(8,128)(2,1)S(1)} copy-done((bf16[4096,1152]{1,0:T(8,128)(2,1)S(1)}, bf16[4096,1152]{1,0:T(8,128)(2,1)}, u32[]{:S(2)}) %copy-start) | copy-done | bytes 9437208
  109.6 6.0 %shard_map.68 = bf16[144,1152]{1,0:T(8,128)(2,1)} custom-call(s32[2]{0:T(128)S(1)} %pad_add_fusion.place, bf16[16,144,256]{2,1,0:T(8,128)(2,1)S(1)} %constant_dynamic-update-slice_fusion.w_ref, bf16[16,256,1152]{2,1,0:T(8,128)(2,1)S(1)} %bitcast.13, bf16[144,1152]{1,0:T(8,128)(2,1)S(1)} %copy-done.1), custom_call_target="tpu_custom_call" | custom-call | flops 1358954496 | bytes 10616832 | tf_op jit(solution)/shard_map/pallas_call | solution.py:70
  (30 shorter events, 0.5 us)
Async XLA Ops:
  7.2 98.7 %all-gather.2.cloned.1.call-start = ((), (), s32[]{:S(2)}) async-start(), calls=%async_computation | async-start | bytes 9732096 | tf_op jit(solution)/shard_map/all_gather | solution.py:95
  8.6 2.6 %copy-start.2 = (bf16[128,1152]{1,0:T(8,128)(2,1)S(1)}, bf16[128,1152]{1,0:T(8,128)(2,1)}, u32[]{:S(2)}) copy-start(bf16[128,1152]{1,0:T(8,128)(2,1)} %param.5) | copy-start | bytes 884740
  12.3 9.6 %collective-permute-start = (f32[8]{0:T(128)S(1)}, f32[8]{0:T(128)S(1)}, u32[]{:S(2)}, u32[]{:S(2)}) collective-permute-start(f32[8]{0:T(128)S(1)} %select_reduce_fusion.1), channel_id=1, source_target_pairs={{0,1},{1,0},{2,3},{3,2},{4,5},{5,4},{6,7},{7,6},{8,9},{9,8},{10,11... | collective-permute-start | bytes 104 | tf_op jit(solution)/shard_map/ppermute | solution.py:26
  14.8 7.2 %collective-permute-start.1 = (f32[8]{0:T(128)S(1)}, f32[8]{0:T(128)S(1)}, u32[]{:S(2)}, u32[]{:S(2)}) collective-permute-start(f32[8]{0:T(128)S(1)} %select_reduce_fusion.1), channel_id=1, source_target_pairs={{0,2},{1,3},{2,0},{3,1},{4,6},{5,7},{6,4},{7,5},{8,10},{9,11},{10,... | collective-permute-start | bytes 104 | tf_op jit(solution)/shard_map/ppermute | solution.py:26
  17.5 5.5 %collective-permute-start.2 = (f32[8]{0:T(128)S(1)}, f32[8]{0:T(128)S(1)}, u32[]{:S(2)}, u32[]{:S(2)}) collective-permute-start(f32[8]{0:T(128)S(1)} %select_reduce_fusion.1), channel_id=1, source_target_pairs={{0,3},{1,2},{2,1},{3,0},{4,7},{5,6},{6,5},{7,4},{8,11},{9,10},{10,... | collective-permute-start | bytes 104 | tf_op jit(solution)/shard_map/ppermute | solution.py:26
  23.0 8.4 %collective-permute-start.3 = (f32[8]{0:T(128)S(1)}, f32[8]{0:T(128)S(1)}, u32[]{:S(2)}, u32[]{:S(2)}) collective-permute-start(f32[8]{0:T(128)S(1)} %add_add_fusion), channel_id=1, source_target_pairs={{0,4},{1,5},{2,6},{3,7},{4,0},{5,1},{6,2},{7,3},{8,12},{9,13},{10,... | collective-permute-start | bytes 104 | tf_op jit(solution)/shard_map/ppermute | solution.py:26
  24.9 6.5 %collective-permute-start.4 = (f32[8]{0:T(128)S(1)}, f32[8]{0:T(128)S(1)}, u32[]{:S(2)}, u32[]{:S(2)}) collective-permute-start(f32[8]{0:T(128)S(1)} %add_add_fusion), channel_id=1, source_target_pairs={{0,8},{1,9},{2,10},{3,11},{4,12},{5,13},{6,14},{7,15},{8,0},{9,1},... | collective-permute-start | bytes 104 | tf_op jit(solution)/shard_map/ppermute | solution.py:26
  29.3 4.7 %collective-permute-start.5 = (f32[8]{0:T(128)S(1)}, f32[8]{0:T(128)S(1)}, u32[]{:S(2)}, u32[]{:S(2)}) collective-permute-start(f32[8]{0:T(128)S(1)} %add_add_fusion), channel_id=1, source_target_pairs={{0,12},{1,13},{2,14},{3,15},{4,8},{5,9},{6,10},{7,11},{8,4},{9,5},... | collective-permute-start | bytes 104 | tf_op jit(solution)/shard_map/ppermute | solution.py:26
  34.6 24.3 %collective-permute-start.6 = (bf16[144,128]{1,0:T(8,128)(2,1)S(1)}, bf16[144,128]{1,0:T(8,128)(2,1)S(1)}, u32[]{:S(2)}, u32[]{:S(2)}) collective-permute-start(bf16[144,128]{1,0:T(8,128)(2,1)S(1)} %get-tuple-element.6), channel_id=1, source_target_pairs={{0,0},{1,33},{2,66},{3,99},{4,132},{5,165},{6,198},{7,231},{8,264}... | collective-permute-start | bytes 110600 | tf_op jit(solution)/shard_map/ppermute | solution.py:118
  47.5 17.3 %collective-permute-start.7 = (bf16[144,128]{1,0:T(8,128)(2,1)S(1)}, bf16[144,128]{1,0:T(8,128)(2,1)S(1)}, u32[]{:S(2)}, u32[]{:S(2)}) collective-permute-start(bf16[144,128]{1,0:T(8,128)(2,1)S(1)} %get-tuple-element.7), channel_id=1, source_target_pairs={{0,16},{1,49},{2,82},{3,115},{4,148},{5,181},{6,214},{7,247},{8,28... | collective-permute-start | bytes 110600 | tf_op jit(solution)/shard_map/ppermute | solution.py:119
  64.8 9.6 %collective-permute-start.10 = (bf16[1,144,256]{2,1,0:T(8,128)(2,1)S(1)}, bf16[1,144,256]{2,1,0:T(8,128)(2,1)S(1)}, u32[]{:S(2)}, u32[]{:S(2)}) collective-permute-start(bf16[1,144,256]{2,1,0:T(8,128)(2,1)S(1)} %maximum_bitcast_fusion), channel_id=1, source_target_pairs={{0,3},{1,2},{2,1},{3,0},{4,7},{5,6},{6,5},{7,4},{8,11},{9,10},{10,... | collective-permute-start | bytes 221192 | tf_op jit(solution)/shard_map/ppermute | solution.py:26
  66.7 7.7 %collective-permute-start.8 = (bf16[1,144,256]{2,1,0:T(8,128)(2,1)S(1)}, bf16[1,144,256]{2,1,0:T(8,128)(2,1)S(1)}, u32[]{:S(2)}, u32[]{:S(2)}) collective-permute-start(bf16[1,144,256]{2,1,0:T(8,128)(2,1)S(1)} %maximum_bitcast_fusion), channel_id=1, source_target_pairs={{0,1},{1,0},{2,3},{3,2},{4,5},{5,4},{6,7},{7,6},{8,9},{9,8},{10,11... | collective-permute-start | bytes 221192 | tf_op jit(solution)/shard_map/ppermute | solution.py:26
  68.7 7.5 %collective-permute-start.9 = (bf16[1,144,256]{2,1,0:T(8,128)(2,1)S(1)}, bf16[1,144,256]{2,1,0:T(8,128)(2,1)S(1)}, u32[]{:S(2)}, u32[]{:S(2)}) collective-permute-start(bf16[1,144,256]{2,1,0:T(8,128)(2,1)S(1)} %maximum_bitcast_fusion), channel_id=1, source_target_pairs={{0,2},{1,3},{2,0},{3,1},{4,6},{5,7},{6,4},{7,5},{8,10},{9,11},{10,... | collective-permute-start | bytes 221192 | tf_op jit(solution)/shard_map/ppermute | solution.py:26
  76.2 29.7 %copy-start.1 = (bf16[144,1152]{1,0:T(8,128)(2,1)S(1)}, bf16[144,1152]{1,0:T(8,128)(2,1)}, u32[]{:S(2)}) copy-start(bf16[144,1152]{1,0:T(8,128)(2,1)} %noise_ref.1) | copy-start | bytes 995332
  76.2 10.3 %collective-permute-start.11 = (bf16[4,144,256]{2,1,0:T(8,128)(2,1)S(1)}, bf16[4,144,256]{2,1,0:T(8,128)(2,1)S(1)}, u32[]{:S(2)}, u32[]{:S(2)}) collective-permute-start(bf16[4,144,256]{2,1,0:T(8,128)(2,1)S(1)} %pad_maximum_fusion), channel_id=1, source_target_pairs={{0,4},{1,5},{2,6},{3,7},{4,0},{5,1},{6,2},{7,3},{8,12},{9,13},{10,... | collective-permute-start | bytes 884744 | tf_op jit(solution)/shard_map/ppermute | solution.py:26
  78.3 13.2 %collective-permute-start.12 = (bf16[4,144,256]{2,1,0:T(8,128)(2,1)S(1)}, bf16[4,144,256]{2,1,0:T(8,128)(2,1)S(1)}, u32[]{:S(2)}, u32[]{:S(2)}) collective-permute-start(bf16[4,144,256]{2,1,0:T(8,128)(2,1)S(1)} %pad_maximum_fusion), channel_id=1, source_target_pairs={{0,8},{1,9},{2,10},{3,11},{4,12},{5,13},{6,14},{7,15},{8,0},{9,1},... | collective-permute-start | bytes 884744 | tf_op jit(solution)/shard_map/ppermute | solution.py:26
  84.6 12.6 %collective-permute-start.13 = (bf16[4,144,256]{2,1,0:T(8,128)(2,1)S(1)}, bf16[4,144,256]{2,1,0:T(8,128)(2,1)S(1)}, u32[]{:S(2)}, u32[]{:S(2)}) collective-permute-start(bf16[4,144,256]{2,1,0:T(8,128)(2,1)S(1)} %pad_maximum_fusion), channel_id=1, source_target_pairs={{0,12},{1,13},{2,14},{3,15},{4,8},{5,9},{6,10},{7,11},{8,4},{9,5},... | collective-permute-start | bytes 884744 | tf_op jit(solution)/shard_map/ppermute | solution.py:26
  105.9 3.7 %copy-start = (bf16[4096,1152]{1,0:T(8,128)(2,1)S(1)}, bf16[4096,1152]{1,0:T(8,128)(2,1)}, u32[]{:S(2)}) copy-start(bf16[4096,1152]{1,0:T(8,128)(2,1)} %all-gather.2.cloned.1.call-done) | copy-start | bytes 28311556
Sparse Core Ops, SparseCore 0:
  10.1 95.7 all-gather.1

commit v2 on v0

v2 whole, which is shorter than its diff:
```python
import jax
import jax.numpy as jnp
from jax import lax
from jax.experimental import pallas as pl
from jax.experimental.pallas import tpu as pltpu
from jax.sharding import Mesh
from jax.sharding import PartitionSpec as P

D = 4608
FFW = 18432
SEQ = 128
NSEG = 8
PLANES = 16
ROW = 4
ROWS = 144

EPSILON = 1e-06
CLIP_FRACTION = 4.2


def clip_bound():
    return CLIP_FRACTION * (FFW * D * NSEG / SEQ) ** 0.5


def along_y(value, distance):
    return lax.ppermute(value, "y", [(i, i ^ distance) for i in range(ROW)])


def fan_out(value, extra, cross):
    perm = []
    for plane in range(PLANES):
        for core in range(2):
            for j in range(ROW * ROW):
                to = ((plane + j + extra) % PLANES) * 2 + (1 - core if cross else core)
                perm.append(((plane * 2 + core) * 16 + j, to * 16 + j))
    return lax.ppermute(value, ("dp", "y", "x"), perm)


def squares_kernel(place, seg_ref, count_ref, hidden_ref, grad_ref, out_ref, count_column_ref, gram_ref):
    step = pl.program_id(0)
    seg = seg_ref[pl.ds(place[0], 1), :]
    row = lax.broadcasted_iota(jnp.int32, (SEQ, SEQ), 0)
    column = lax.broadcasted_iota(jnp.int32, (SEQ, SEQ), 1)

    @pl.when(step == 0)
    def _():
        count = jnp.zeros((1, SEQ), jnp.float32)
        for i in range(NSEG):
            count = jnp.where(seg == i, count_ref[i].astype(jnp.float32), count)
        count_column_ref[...] = jnp.sum(jnp.where(row == column, count, 0.0), axis=1, keepdims=True)
        gram_ref[...] = jnp.zeros_like(gram_ref)

    contract = (((1,), (1,)), ((), ()))
    scaled = (grad_ref[...].astype(jnp.float32) / count_column_ref[...]).astype(jnp.bfloat16)
    gram_ref[...] += lax.dot_general(scaled, scaled, contract, preferred_element_type=jnp.float32)

    @pl.when(step == pl.num_programs(0) - 1)
    def _():
        gram_hidden = lax.dot_general(
            hidden_ref[...], hidden_ref[...], contract, preferred_element_type=jnp.float32
        )
        seg_wide = seg.astype(jnp.float32)
        seg_column = jnp.sum(jnp.where(row == column, seg_wide, 0.0), axis=1, keepdims=True)
        products = jnp.where(seg_column == seg_wide, gram_hidden * gram_ref[...], 0.0)
        columns = jnp.sum(products, axis=0, keepdims=True)
        example = lax.broadcasted_iota(jnp.int32, (NSEG, SEQ), 0)
        total = jnp.sum(jnp.where(example == seg, columns, 0.0), axis=1, keepdims=True)
        out_ref[...] = jnp.broadcast_to(total, (NSEG, SEQ))


def partial_squares(dp, seg_rows, counts, hidden, grad_out):
    width = 1536
    return pl.pallas_call(
        squares_kernel,
        grid_spec=pltpu.PrefetchScalarGridSpec(
            num_scalar_prefetch=1,
            grid=(D // width,),
            in_specs=[
                pl.BlockSpec(seg_rows.shape, lambda k, p: (0, 0)),
                pl.BlockSpec(memory_space=pltpu.SMEM),
                pl.BlockSpec(hidden.shape, lambda k, p: (0, 0)),
                pl.BlockSpec((SEQ, width), lambda k, p: (0, k)),
            ],
            out_specs=pl.BlockSpec((NSEG, SEQ), lambda k, p: (0, 0)),
            scratch_shapes=[pltpu.VMEM((SEQ, 1), jnp.float32), pltpu.VMEM((SEQ, SEQ), jnp.float32)],
        ),
        out_shape=jax.ShapeDtypeStruct((NSEG, SEQ), jnp.float32),
        compiler_params=pltpu.CompilerParams(vmem_limit_bytes=56 * 1024 * 1024),
    )(dp[None], seg_rows, counts, hidden, grad_out)


def order_kernel(place, *refs):
    quarters, out_ref = refs[:ROW], refs[ROW]
    for i in range(2 * PLANES):
        for k in range(ROW):

            @pl.when(place[0, i] == k)
            def _(i=i, k=k):
                out_ref[:, i * SEQ : (i + 1) * SEQ] = quarters[k][place[1, i]]


def in_order(place, quarters):
    vmem = pl.BlockSpec(memory_space=pltpu.VMEM)
    return pl.pallas_call(
        order_kernel,
        in_specs=[pl.BlockSpec(memory_space=pltpu.SMEM)] + [vmem] * ROW,
        out_specs=vmem,
        out_shape=jax.ShapeDtypeStruct((ROWS, 2 * PLANES * SEQ), jnp.bfloat16),
        compiler_params=pltpu.CompilerParams(vmem_limit_bytes=24 * 1024 * 1024),
    )(place, *quarters)


def per_device(hidden, grad_out, seg_ids, seg_counts, added_noise):
    dp = lax.axis_index("dp")
    x, y = lax.axis_index("x"), lax.axis_index("y")
    plane, core, j = dp // 2, dp % 2, y * ROW + x
    h_all = lax.all_gather(hidden, "dp", axis=0, tiled=True)

    seg_rows = seg_ids.reshape(-1, SEQ)
    member = lax.dynamic_slice_in_dim(seg_rows, dp, 1, 0) == jnp.arange(NSEG, dtype=jnp.int32)[:, None]

    def per_token(values):
        return jnp.sum(jnp.where(member, values[:, None], 0.0), axis=0, keepdims=True)

    counts = per_token(seg_counts.astype(jnp.float32))
    squares = partial_squares(dp, seg_rows, seg_counts, hidden, grad_out)

    def piece(target, of_core):
        start = (target % PLANES * 2 + of_core) * ROWS
        block = lax.dynamic_slice_in_dim(grad_out, start, ROWS, 1).T
        return (block.astype(jnp.float32) / counts).astype(jnp.bfloat16)

    keep, swap = piece(plane + j, core), piece(plane + j + 8, 1 - core)
    keep, swap, squares = lax.optimization_barrier((keep, swap, squares))
    norms = jnp.sqrt(lax.psum(lax.psum(squares, "x"), "y")[:, 0] + EPSILON)
    factor = per_token(jnp.minimum(1.0, clip_bound() / norms))

    def weighted(scaled):
        return (scaled.astype(jnp.float32) * factor).astype(jnp.bfloat16)

    keep, swap = fan_out(weighted(keep), 0, False), fan_out(weighted(swap), 8, True)
    row = lax.all_gather(jnp.stack([keep, swap]), "x", axis=0, tiled=True)
    quarters = [row] + [along_y(row, k) for k in range(1, ROW)]

    sequence = jnp.arange(2 * PLANES)
    other = (sequence % 2 != core).astype(jnp.int32)
    came = (plane - sequence // 2 + 2 * PLANES - 8 * other) % PLANES
    place = jnp.stack([(came // ROW) ^ y, (came % ROW) * 2 + other]).astype(jnp.int32)
    w_rows = in_order(place, quarters)
    summed = jnp.dot(w_rows, h_all, preferred_element_type=jnp.float32)
    weight_grad = (summed + added_noise.astype(jnp.float32)).astype(jnp.bfloat16)
    return (weight_grad, norms)


def solution(mesh):
    split = Mesh(mesh.devices.reshape(-1, ROW, ROW), ("dp", "y", "x"))
    tensor = ("y", "x")
    placed = (P("dp", tensor), P("dp", None), P(), P("dp"), P("dp", tensor))
    return jax.shard_map(
        per_device,
        mesh=split,
        in_specs=placed,
        out_specs=(P("dp", tensor), P("dp")),
        check_vma=False,
    )
```

time: 157 us -> 114 us (0.73); the launches traced: 157 us -> 112 us
  blocking collectives: 130 us -> 31.5 us
  starting transfers between devices: 0.04 us -> 30.4 us
  waiting for transfers between devices: 1.77 us -> 20.2 us
  Pallas kernels: 0 us -> 5.74 us
    all_to_all x1 -> x0, blocking collectives: 96.1 us -> none  [per_device(): lax.all_to_all(weighted_rows, 'dp', split_axis=1, concat_axis=0, tiled=True)]
    ppermute x0 -> x5, starting transfers between devices: none -> 30.3 us  [the longest x2 20.7 us: fan_out(): return lax.ppermute(value, ('dp', 'y', 'x'), perm)]
    psum x1 -> x2, blocking collectives: 34.3 us -> 18.1 us  [per_device(): norms = jnp.sqrt(lax.psum(lax.psum(squares, 'x'), 'y')[:, 0] + EPSILON)]
    all_gather x0 -> x1, blocking collectives: none -> 13.4 us  [per_device(): row = lax.all_gather(jnp.stack([keep, swap]), 'x', axis=0, tiled=True)]
    ppermute x0 -> x5, waiting for transfers between devices: none -> 12.6 us  [the longest x3 10.2 us: along_y(): return lax.ppermute(value, 'y', [(i, i ^ distance) for i in range(ROW)])]
    all_gather x1, waiting for transfers between devices: 1.09 us -> 6.87 us  [per_device(): h_all = lax.all_gather(hidden, 'dp', axis=0, tiled=True)]
    pallas_call x0 -> x2, Pallas kernels: none -> 5.74 us  [the longest x1 3.88 us: partial_squares(): pl.pallas_call(squares_kernel, grid_spec=pltpu.PrefetchScalarGridSpec(num...]
    unnamed x9 -> x4, local copies, waits for them, and re-layouts: 1.81 us -> 0.23 us
  transfers between devices with their start and end apart: 1 -> 6, of which waited for: 1 -> 4; matrix products, arithmetic and copies ran while one was open for 3% -> 3% of each run, Pallas kernels for 0% -> 5%
where the time goes in v2:
time: 114 us; the launch traced here: 112 us
  blocking collectives  31.5 us (28%)
  starting transfers between devices  30.4 us (27%)
  waiting for transfers between devices  20.2 us (18%)
  between operations  14.2 us (12%)
  matrix products  6.12 us (5%)
  Pallas kernels  5.74 us (5%)
  local copies, waits for them, and re-layouts  1.97 us (2%)
  other arithmetic  1.57 us (1%)
    ppermute x2, starting transfers between devices, fan_out(): return lax.ppermute(value, ('dp', 'y', 'x'), perm)  20.7 us
    psum x2, blocking collectives, per_device(): norms = jnp.sqrt(lax.psum(lax.psum(squares, 'x'), 'y')[:, 0] + EPSILON)  18.1 us
    all_gather x1, blocking collectives, per_device(): row = lax.all_gather(jnp.stack([keep, swap]), 'x', axis=0, tiled=True)  13.4 us
    ppermute x3, waiting for transfers between devices, along_y(): return lax.ppermute(value, 'y', [(i, i ^ distance) for i in range(ROW)])  10.2 us
    ppermute x3, starting transfers between devices, along_y(): return lax.ppermute(value, 'y', [(i, i ^ distance) for i in range(ROW)])  9.57 us
    all_gather x1, waiting for transfers between devices, per_device(): h_all = lax.all_gather(hidden, 'dp', axis=0, tiled=True)  6.87 us
    dot_general x1, matrix products, per_device(): summed = jnp.dot(w_rows, h_all, preferred_element_type=jnp.float32)  6.12 us
    pallas_call x1, Pallas kernels, partial_squares(): pl.pallas_call(squares_kernel, grid_spec=pltpu.PrefetchScalarGridSpec(num...  3.88 us
  transfers between devices with their start and end apart: 6, of which 4 were waited for; matrix products, arithmetic and copies ran while one was open for 3% of the time, Pallas kernels for 5%

profile of v2, /device:TPU:1, one launch (start us, length us, event | category | flops | bytes accessed | tf_op | source)
XLA Modules:
  0.0 111.6 jit_solution(7211841308661625936)
XLA Ops:
  7.2 0.0 all-gather.2.cloned.1.call-start
  7.2 0.7 all-gather.2.cloned.1.call-update
  8.0 1.1 constant_dynamic-slice_fusion
  9.0 0.1 copy.15
  9.1 0.1 copy.16
  9.3 0.7 convert_element_type.53
  9.9 3.9 %shard_map.68 = f32[8,128]{1,0:T(8,128)} custom-call(s32[1]{0:T(128)} %bitcast.4.place, s32[32,128]{1,0:T(8,128)} %bitcast.14, s32[8]{0:T(128)} %count_ref.1, bf16[128,1152]{1,0:T(8,128)(2,1)} %hidden_ref.1, bf16[128,4608]{1,0:T(8,128)(2,1)} %grad_ref.1), custom_call_target="tpu_custom_call" | custom-call | tf_op jit(solution)/shard_map/pallas_call | solution.py:73
  13.8 0.7 fusion.3
  14.5 0.1 select_reduce_fusion.1
  14.6 9.4 %psum.14 = f32[8,128]{1,0:T(8,128)S(1)} all-reduce(f32[8,128]{1,0:T(8,128)} %shard_map.68), channel_id=1, replica_groups=mesh['dp'=32,'y'=4,'x'=4] {'x'}, use_global_device_ids=true, to_apply=%region_1.2 | all-reduce | flops 1024 | bytes 8192 | tf_op jit(solution)/shard_map/psum | solution.py:135
  24.0 8.7 %psum.15 = f32[8,128]{1,0:T(8,128)S(1)} all-reduce(f32[8,128]{1,0:T(8,128)S(1)} %psum.14), channel_id=1, replica_groups=mesh['dp'=32,'y'=4,'x'=4] {'y'}, use_global_device_ids=true, to_apply=%region_2.3 | all-reduce | flops 1024 | bytes 8192 | tf_op jit(solution)/shard_map/psum | solution.py:135
  32.7 0.6 sqrt_reduce_fusion
  33.4 0.1 select_reduce_fusion
  33.5 0.7 collective-permute-start
  34.1 20.1 %collective-permute-start.1 = (bf16[144,128]{1,0:T(8,128)(2,1)S(1)}, bf16[144,128]{1,0:T(8,128)(2,1)S(1)}, u32[]{:S(2)}, u32[]{:S(2)}) collective-permute-start(bf16[144,128]{1,0:T(8,128)(2,1)S(1)} %get-tuple-element.13), channel_id=1, source_target_pairs={{0,272},{1,305},{2,338},{3,371},{4,404},{5,437},{6,470},{7,503},{8... | collective-permute-start | bytes 110600 | tf_op jit(solution)/shard_map/ppermute | solution.py:36
  54.2 0.0 collective-permute-done
  54.2 2.4 %collective-permute-done.1 = bf16[144,128]{1,0:T(8,128)(2,1)S(1)} collective-permute-done((bf16[144,128]{1,0:T(8,128)(2,1)S(1)}, bf16[144,128]{1,0:T(8,128)(2,1)S(1)}, u32[]{:S(2)}, u32[]{:S(2)}) %collective-permute-start.1) | collective-permute-done | bytes 36896 | tf_op jit(solution)/shard_map/ppermute | solution.py:36
  56.7 13.4 %all_gather.6.refs_0_ = bf16[8,144,128]{2,1,0:T(8,128)(2,1)S(1)} all-gather(bf16[2,144,128]{2,1,0:T(8,128)(2,1)S(1)} %pad_maximum_fusion), channel_id=1, replica_groups=mesh['dp'=32,'y'=4,'x'=4] {'x'}, dimensions={0}, use_global_device_ids=true | all-gather | bytes 368640 | tf_op jit(solution)/shard_map/all_gather | solution.py:142
  70.1 1.9 %collective-permute-start.2 = (bf16[8,144,128]{2,1,0:T(8,128)(2,1)S(1)}, bf16[8,144,128]{2,1,0:T(8,128)(2,1)S(1)}, u32[]{:S(2)}, u32[]{:S(2)}) collective-permute-start(bf16[8,144,128]{2,1,0:T(8,128)(2,1)S(1)} %all_gather.6.refs_0_), channel_id=1, source_target_pairs={{0,4},{4,0},{8,12},{12,8},{1,5},{5,1},{9,13},{13,9},{2,6},{6,2},{1... | collective-permute-start | bytes 884744 | tf_op jit(solution)/shard_map/ppermute | solution.py:26
  72.0 2.1 %collective-permute-start.3 = (bf16[8,144,128]{2,1,0:T(8,128)(2,1)S(1)}, bf16[8,144,128]{2,1,0:T(8,128)(2,1)S(1)}, u32[]{:S(2)}, u32[]{:S(2)}) collective-permute-start(bf16[8,144,128]{2,1,0:T(8,128)(2,1)S(1)} %all_gather.6.refs_0_), channel_id=1, source_target_pairs={{0,8},{4,12},{8,0},{12,4},{1,9},{5,13},{9,1},{13,5},{2,10},{6,14},... | collective-permute-start | bytes 884744 | tf_op jit(solution)/shard_map/ppermute | solution.py:26
  74.1 5.5 %collective-permute-start.4 = (bf16[8,144,128]{2,1,0:T(8,128)(2,1)S(1)}, bf16[8,144,128]{2,1,0:T(8,128)(2,1)S(1)}, u32[]{:S(2)}, u32[]{:S(2)}) collective-permute-start(bf16[8,144,128]{2,1,0:T(8,128)(2,1)S(1)} %all_gather.6.refs_0_), channel_id=1, source_target_pairs={{0,12},{4,8},{8,4},{12,0},{1,13},{5,9},{9,5},{13,1},{2,14},{6,10},... | collective-permute-start | bytes 884744 | tf_op jit(solution)/shard_map/ppermute | solution.py:26
  79.7 0.0 copy-start
  79.7 0.0 collective-permute-done.2.refs_1_
  79.7 3.7 %collective-permute-done.3.refs_2_ = bf16[8,144,128]{2,1,0:T(8,128)(2,1)S(1)} collective-permute-done((bf16[8,144,128]{2,1,0:T(8,128)(2,1)S(1)}, bf16[8,144,128]{2,1,0:T(8,128)(2,1)S(1)}, u32[]{:S(2)}, u32[]{:S(2)}) %collective-permute-start.3) | collective-permute-done | bytes 294944 | tf_op jit(solution)/shard_map/ppermute | solution.py:26
  83.5 6.5 %collective-permute-done.4.refs_3_ = bf16[8,144,128]{2,1,0:T(8,128)(2,1)S(1)} collective-permute-done((bf16[8,144,128]{2,1,0:T(8,128)(2,1)S(1)}, bf16[8,144,128]{2,1,0:T(8,128)(2,1)S(1)}, u32[]{:S(2)}, u32[]{:S(2)}) %collective-permute-start.4) | collective-permute-done | bytes 294944 | tf_op jit(solution)/shard_map/ppermute | solution.py:26
  89.9 1.9 %shard_map.69 = bf16[144,4096]{1,0:T(8,128)(2,1)S(1)} custom-call(s32[2,32]{1,0:T(2,128)S(1)} %pad_add_fusion.place, bf16[8,144,128]{2,1,0:T(8,128)(2,1)S(1)} %all_gather.6.refs_0_, bf16[8,144,128]{2,1,0:T(8,128)(2,1)S(1)} %collective-permute-done.2.refs_1_, bf16[8,144,128]{2,1,0:T(8,128)(2,1)S(1)} %collective-permute-done.3.refs_2_, ...), custom_call_target="tpu_custom_call" | custom-call | tf_op jit(solution)/shard_map/pallas_call | solution.py:104
  91.8 6.9 %all-gather.2.cloned.1.call-done = bf16[4096,1152]{1,0:T(8,128)(2,1)} async-done(((bf16[128,1152]{1,0:T(8,128)(2,1)}), bf16[4096,1152]{1,0:T(8,128)(2,1)}) %all-gather.2.cloned.1.call-update) | async-done | bytes 9437200 | tf_op jit(solution)/shard_map/all_gather | solution.py:117
  98.7 0.0 copy-done
  98.7 6.1 %fusion = bf16[144,1152]{1,0:T(8,128)(2,1)} fusion(bf16[144,4096]{1,0:T(8,128)(2,1)S(1)} %shard_map.69, bf16[4096,1152]{1,0:T(8,128)(2,1)} %all-gather.2.cloned.1.call-done, bf16[144,1152]{1,0:T(8,128)(2,1)S(1)} %copy-done), kind=kOutput, calls=%fused_computation.1 | convolution fusion | flops 1359452160 | bytes 11280384 | tf_op jit(solution)/shard_map/dot_general | solution.py:150
  (5 shorter events, 0.1 us)
Async XLA Ops:
  7.2 91.5 %all-gather.2.cloned.1.call-start = ((), (), s32[]{:S(2)}) async-start(), calls=%async_computation | async-start | bytes 9732096 | tf_op jit(solution)/shard_map/all_gather | solution.py:117
  33.5 20.8 %collective-permute-start = (bf16[144,128]{1,0:T(8,128)(2,1)S(1)}, bf16[144,128]{1,0:T(8,128)(2,1)S(1)}, u32[]{:S(2)}, u32[]{:S(2)}) collective-permute-start(bf16[144,128]{1,0:T(8,128)(2,1)S(1)} %get-tuple-element.12), channel_id=1, source_target_pairs={{0,0},{1,33},{2,66},{3,99},{4,132},{5,165},{6,198},{7,231},{8,264}... | collective-permute-start | bytes 110600 | tf_op jit(solution)/shard_map/ppermute | solution.py:36
  34.1 22.5 %collective-permute-start.1 = (bf16[144,128]{1,0:T(8,128)(2,1)S(1)}, bf16[144,128]{1,0:T(8,128)(2,1)S(1)}, u32[]{:S(2)}, u32[]{:S(2)}) collective-permute-start(bf16[144,128]{1,0:T(8,128)(2,1)S(1)} %get-tuple-element.13), channel_id=1, source_target_pairs={{0,272},{1,305},{2,338},{3,371},{4,404},{5,437},{6,470},{7,503},{8... | collective-permute-start | bytes 110600 | tf_op jit(solution)/shard_map/ppermute | solution.py:36
  70.1 9.7 %collective-permute-start.2 = (bf16[8,144,128]{2,1,0:T(8,128)(2,1)S(1)}, bf16[8,144,128]{2,1,0:T(8,128)(2,1)S(1)}, u32[]{:S(2)}, u32[]{:S(2)}) collective-permute-start(bf16[8,144,128]{2,1,0:T(8,128)(2,1)S(1)} %all_gather.6.refs_0_), channel_id=1, source_target_pairs={{0,4},{4,0},{8,12},{12,8},{1,5},{5,1},{9,13},{13,9},{2,6},{6,2},{1... | collective-permute-start | bytes 884744 | tf_op jit(solution)/shard_map/ppermute | solution.py:26
  72.0 11.5 %collective-permute-start.3 = (bf16[8,144,128]{2,1,0:T(8,128)(2,1)S(1)}, bf16[8,144,128]{2,1,0:T(8,128)(2,1)S(1)}, u32[]{:S(2)}, u32[]{:S(2)}) collective-permute-start(bf16[8,144,128]{2,1,0:T(8,128)(2,1)S(1)} %all_gather.6.refs_0_), channel_id=1, source_target_pairs={{0,8},{4,12},{8,0},{12,4},{1,9},{5,13},{9,1},{13,5},{2,10},{6,14},... | collective-permute-start | bytes 884744 | tf_op jit(solution)/shard_map/ppermute | solution.py:26
  74.1 15.8 %collective-permute-start.4 = (bf16[8,144,128]{2,1,0:T(8,128)(2,1)S(1)}, bf16[8,144,128]{2,1,0:T(8,128)(2,1)S(1)}, u32[]{:S(2)}, u32[]{:S(2)}) collective-permute-start(bf16[8,144,128]{2,1,0:T(8,128)(2,1)S(1)} %all_gather.6.refs_0_), channel_id=1, source_target_pairs={{0,12},{4,8},{8,4},{12,0},{1,13},{5,9},{9,5},{13,1},{2,14},{6,10},... | collective-permute-start | bytes 884744 | tf_op jit(solution)/shard_map/ppermute | solution.py:26
  79.7 19.0 %copy-start = (bf16[144,1152]{1,0:T(8,128)(2,1)S(1)}, bf16[144,1152]{1,0:T(8,128)(2,1)}, u32[]{:S(2)}) copy-start(bf16[144,1152]{1,0:T(8,128)(2,1)} %param.9) | copy-start | bytes 995332
Sparse Core Ops, SparseCore 0:
  10.1 88.5 all-gather.1

commit v3 on v0

v3 whole, which is shorter than its diff:
```python
import functools

import jax
import jax.numpy as jnp
from jax import lax
from jax.experimental import pallas as pl
from jax.experimental.pallas import tpu as pltpu
from jax.sharding import Mesh
from jax.sharding import PartitionSpec as P

D = 4608
FFW = 18432
SEQ = 128
NSEG = 8
PLANES = 16
PAIRS = PLANES // 2
ROW = 4
ROWS = 144

EPSILON = 1e-06
CLIP_FRACTION = 4.2


def clip_bound():
    return CLIP_FRACTION * (FFW * D * NSEG / SEQ) ** 0.5


def along_y(value, distance):
    return lax.ppermute(value, "y", [(i, i ^ distance) for i in range(ROW)])


def fan_out(value, extra, cross):
    perm = []
    for plane in range(PLANES):
        for core in range(2):
            for j in range(ROW * ROW):
                to = ((plane + 2 * (j % PAIRS + extra)) % PLANES) * 2 + (1 - core if cross else core)
                perm.append(((plane * 2 + core) * 16 + j, to * 16 + j))
    return lax.ppermute(value, ("pair", "parity", "core", "y", "x"), perm)


def to_neighbour(value):
    perm = [(plane * 2 + core, (plane + 1 - 2 * core) % PLANES * 2 + core) for plane in range(PLANES) for core in range(2)]
    return lax.ppermute(value, ("pair", "parity", "core"), perm)


def squares_kernel(place, seg_ref, count_ref, hidden_ref, grad_ref, out_ref, keep_ref, swap_ref, turned_ref):
    seg = seg_ref[pl.ds(place[0], 1), :]
    row = lax.broadcasted_iota(jnp.int32, (SEQ, SEQ), 0)
    column = lax.broadcasted_iota(jnp.int32, (SEQ, SEQ), 1)
    count = jnp.zeros((1, SEQ), jnp.float32)
    for i in range(NSEG):
        count = jnp.where(seg == i, count_ref[i].astype(jnp.float32), count)
    count_column = jnp.sum(jnp.where(row == column, count, 0.0), axis=1, keepdims=True)

    def scaled(block):
        return (block.astype(jnp.float32) / count_column).astype(jnp.bfloat16)

    contract = (((1,), (1,)), ((), ()))
    gram_hidden = lax.dot_general(
        hidden_ref[...], hidden_ref[...], contract, preferred_element_type=jnp.float32
    )
    gram_scaled = jnp.zeros((SEQ, SEQ), jnp.float32)
    width = 512
    for k in range(D // width):
        block = scaled(grad_ref[:, k * width : (k + 1) * width])
        gram_scaled += lax.dot_general(block, block, contract, preferred_element_type=jnp.float32)
    seg_wide = seg.astype(jnp.float32)
    seg_column = jnp.sum(jnp.where(row == column, seg_wide, 0.0), axis=1, keepdims=True)
    products = jnp.where(seg_column == seg_wide, gram_hidden * gram_scaled, 0.0)
    columns = jnp.sum(products, axis=0, keepdims=True)
    example = lax.broadcasted_iota(jnp.int32, (NSEG, SEQ), 0)
    total = jnp.sum(jnp.where(example == seg, columns, 0.0), axis=1, keepdims=True)
    of_token = jnp.sum(jnp.where(example == seg, total, 0.0), axis=0, keepdims=True)
    out_ref[:NSEG, :] = jnp.broadcast_to(total, (NSEG, SEQ))
    out_ref[NSEG:, :] = jnp.broadcast_to(of_token, (NSEG, SEQ))

    window = turned_ref.shape[0]
    for n, piece_ref in enumerate((keep_ref, swap_ref)):
        start = place[1 + n]
        at = pl.multiple_of(jnp.minimum(start // SEQ * SEQ, D - window), SEQ)
        turned_ref[...] = scaled(grad_ref[:, pl.ds(at, window)]).astype(jnp.float32).T
        inside = pl.multiple_of(start - at, 16)
        piece_ref[...] = turned_ref[pl.ds(inside, ROWS), :].astype(jnp.bfloat16)


def partial_squares(place, seg_rows, counts, hidden, grad_out):
    vmem, smem = pl.BlockSpec(memory_space=pltpu.VMEM), pl.BlockSpec(memory_space=pltpu.SMEM)
    piece = jax.ShapeDtypeStruct((ROWS, SEQ), jnp.bfloat16)
    return pl.pallas_call(
        squares_kernel,
        in_specs=[smem, vmem, smem, vmem, vmem],
        out_specs=[vmem] * 3,
        out_shape=[jax.ShapeDtypeStruct((2 * NSEG, SEQ), jnp.float32), piece, piece],
        scratch_shapes=[pltpu.VMEM((3 * SEQ, SEQ), jnp.float32)],
        compiler_params=pltpu.CompilerParams(vmem_limit_bytes=56 * 1024 * 1024),
    )(place, seg_rows, counts, hidden, grad_out)


def product_kernel(own, place, *refs):
    quarters, h_ref, rest = refs[:ROW], refs[ROW], refs[ROW + 1 :]
    out_ref, w_ref = rest[-2], rest[-1]
    for i in range(PLANES):
        for k in range(ROW):

            @pl.when(place[0, i] == k)
            def _(i=i, k=k):
                w_ref[:, i * SEQ : (i + 1) * SEQ] = quarters[k][place[1, i]]

    summed = jnp.dot(w_ref[...], h_ref[...], preferred_element_type=jnp.float32)
    if own:
        summed += rest[0][...].astype(jnp.float32)
    out_ref[...] = summed.astype(out_ref.dtype)


def product(place, quarters, h_all, noise=None):
    own = noise is not None
    tokens, columns = h_all.shape
    vmem = pl.BlockSpec(memory_space=pltpu.VMEM)
    return pl.pallas_call(
        functools.partial(product_kernel, own),
        in_specs=[pl.BlockSpec(memory_space=pltpu.SMEM)] + [vmem] * (ROW + 1 + own),
        out_specs=vmem,
        out_shape=jax.ShapeDtypeStruct((ROWS, columns), jnp.float32 if own else jnp.bfloat16),
        scratch_shapes=[pltpu.VMEM((ROWS, tokens), jnp.bfloat16)],
        compiler_params=pltpu.CompilerParams(vmem_limit_bytes=24 * 1024 * 1024),
        cost_estimate=pl.CostEstimate(
            flops=2 * tokens * ROWS * columns, bytes_accessed=2 * tokens * (ROWS + columns), transcendentals=0
        ),
    )(place, *quarters, h_all, *([noise] if own else []))


def per_device(hidden, grad_out, seg_ids, seg_counts, added_noise):
    pair, parity, core = lax.axis_index("pair"), lax.axis_index("parity"), lax.axis_index("core")
    x, y = lax.axis_index("x"), lax.axis_index("y")
    plane, j = pair * 2 + parity, y * ROW + x
    dp = plane * 2 + core
    h_all = lax.all_gather(hidden, ("pair", "core"), axis=0, tiled=True)

    seg_rows = seg_ids.reshape(-1, SEQ)

    def start(to_plane, of_core):
        shift = jnp.where(y < 2, 0, 1 - 2 * of_core)
        return ((to_plane + shift + PLANES) % PLANES * 2 + of_core) * ROWS

    ahead = plane + 2 * (j % PAIRS)
    here = jnp.stack([dp, start(ahead, core), start(ahead + 8, 1 - core)]).astype(jnp.int32)
    squares, keep, swap = partial_squares(here, seg_rows, seg_counts, hidden, grad_out)
    squares = lax.psum(lax.psum(squares, "x"), "y")
    norms = jnp.sqrt(squares[:NSEG, 0] + EPSILON)
    factor = jnp.minimum(1.0, clip_bound() / jnp.sqrt(squares[NSEG : NSEG + 1] + EPSILON))

    def weighted(scaled):
        return (scaled.astype(jnp.float32) * factor).astype(jnp.bfloat16)

    keep, swap = fan_out(weighted(keep), 0, False), fan_out(weighted(swap), 4, True)
    row = lax.all_gather(jnp.stack([keep, swap]), "x", axis=0, tiled=True)
    one, two, three = [along_y(row, k) for k in range(1, ROW)]
    h_all, three = lax.optimization_barrier((h_all, three))
    quarters = [row, one, two, three]

    sequence = jnp.arange(PLANES)
    other = (sequence % 2 != core).astype(jnp.int32)
    came = (pair - sequence // 2 + 2 * PAIRS - 4 * other) % PAIRS
    inside = came % ROW * 2 + other

    def place(block):
        return jnp.stack([(2 * block + came // ROW) ^ y, inside]).astype(jnp.int32)

    handed = to_neighbour(product(place(1), quarters, h_all))
    summed = product(place(0), quarters, h_all, added_noise)
    weight_grad = (summed + handed.astype(jnp.float32)).astype(jnp.bfloat16)
    return (weight_grad, norms)


def solution(mesh):
    split = Mesh(mesh.devices.reshape(PAIRS, 2, 2, ROW, ROW), ("pair", "parity", "core", "y", "x"))
    dp, tensor = ("pair", "parity", "core"), ("y", "x")
    placed = (P(dp, tensor), P(dp, None), P(), P(dp), P(dp, tensor))
    return jax.shard_map(
        per_device,
        mesh=split,
        in_specs=placed,
        out_specs=(P(dp, tensor), P(dp)),
        check_vma=False,
    )
```

time: 157 us -> 113 us (0.72)
  the two profiles are of different devices: /device:TPU:1 before, /device:TPU:30 now
where the time goes in v3:
time: 113 us; the launch traced here: 112 us
  waiting for transfers between devices  32.7 us (29%)
  blocking collectives  31.7 us (28%)
  starting transfers between devices  21.4 us (19%)
  between operations  14.2 us (13%)
  Pallas kernels  7.08 us (6%)
  other arithmetic  2.88 us (3%)
  local copies, waits for them, and re-layouts  2.35 us (2%)
    psum x2, blocking collectives, per_device(): squares = lax.psum(lax.psum(squares, 'x'), 'y')  19.4 us
    ppermute x2, waiting for transfers between devices, fan_out(): return lax.ppermute(value, ('pair', 'parity', 'core', 'y', 'x'), perm)  14.8 us
    all_gather x1, blocking collectives, per_device(): row = lax.all_gather(jnp.stack([keep, swap]), 'x', axis=0, tiled=True)  12.3 us
    ppermute x3, starting transfers between devices, along_y(): return lax.ppermute(value, 'y', [(i, i ^ distance) for i in range(ROW)])  9.81 us
    ppermute x2, starting transfers between devices, fan_out(): return lax.ppermute(value, ('pair', 'parity', 'core', 'y', 'x'), perm)  9.6 us
    all_gather x1, waiting for transfers between devices, per_device(): h_all = lax.all_gather(hidden, ('pair', 'core'), axis=0, tiled=True)  7.64 us
    ppermute x1, waiting for transfers between devices, to_neighbour(): return lax.ppermute(value, ('pair', 'parity', 'core'), perm)  5.5 us
    pallas_call x2, Pallas kernels, product(): pl.pallas_call(functools.partial(product_kernel, own), in_specs=[pl.Block...  4.29 us
  transfers between devices with their start and end apart: 7, of which 4 were waited for; matrix products, arithmetic and copies ran while one was open for 2% of the time, Pallas kernels for 4%

profile of v3, /device:TPU:30, one launch (start us, length us, event | category | flops | bytes accessed | tf_op | source)
XLA Modules:
  0.0 112.3 jit_solution(6673526344806405791)
XLA Ops:
  7.2 0.0 copy-start.2
  7.2 0.0 all-gather.2.cloned.1.call-start
  7.2 0.7 all-gather.2.cloned.1.call-update
  8.0 0.6 pad_add_fusion.2.place
  8.5 2.8 %shard_map.68 = (f32[16,128]{1,0:T(8,128)}, bf16[144,128]{1,0:T(8,128)(2,1)}, bf16[144,128]{1,0:T(8,128)(2,1)}) custom-call(s32[3]{0:T(128)} %pad_add_fusion.2.place, s32[32,128]{1,0:T(8,128)} %bitcast.10, s32[8]{0:T(128)} %count_ref.1, bf16[128,1152]{1,0:T(8,128)(2,1)} %hidden_ref.1, bf16[128,4608]{1,0:T(8,128)(2,1)} %grad_ref.1), custom_call_target="tpu_custom_call" | custom-call | tf_op jit(solution)/shard_map/pallas_call | solution.py:90
  11.3 7.7 %psum.14 = f32[16,128]{1,0:T(8,128)S(1)} all-reduce(f32[16,128]{1,0:T(8,128)} %get-tuple-element.8), channel_id=1, replica_groups=mesh['pair'=8,'parity'=2,'core'=2,'y'=4,'x'=4] {'x'}, use_global_device_ids=true, to_apply=%region_0.1 | all-reduce | flops 2048 | bytes 16384 | tf_op jit(solution)/shard_map/psum | solution.py:149
  19.0 11.7 %psum.15 = f32[16,128]{1,0:T(8,128)S(1)} all-reduce(f32[16,128]{1,0:T(8,128)S(1)} %psum.14), channel_id=1, replica_groups=mesh['pair'=8,'parity'=2,'core'=2,'y'=4,'x'=4] {'y'}, use_global_device_ids=true, to_apply=%region_1.2 | all-reduce | flops 2048 | bytes 16384 | tf_op jit(solution)/shard_map/psum | solution.py:149
  30.8 0.8 multiply_convert_fusion.1
  31.6 7.7 %collective-permute-start = (bf16[144,128]{1,0:T(8,128)(2,1)S(1)}, bf16[144,128]{1,0:T(8,128)(2,1)S(1)}, u32[]{:S(2)}, u32[]{:S(2)}) collective-permute-start(bf16[144,128]{1,0:T(8,128)(2,1)S(1)} %get-tuple-element.14), channel_id=1, source_target_pairs={{0,0},{1,65},{2,130},{3,195},{4,260},{5,325},{6,390},{7,455},{8,8}... | collective-permute-start | bytes 110600 | tf_op jit(solution)/shard_map/ppermute | solution.py:39
  39.3 1.9 %collective-permute-start.1 = (bf16[144,128]{1,0:T(8,128)(2,1)S(1)}, bf16[144,128]{1,0:T(8,128)(2,1)S(1)}, u32[]{:S(2)}, u32[]{:S(2)}) collective-permute-start(bf16[144,128]{1,0:T(8,128)(2,1)S(1)} %get-tuple-element.15), channel_id=1, source_target_pairs={{0,272},{1,337},{2,402},{3,467},{4,20},{5,85},{6,150},{7,215},{8,2... | collective-permute-start | bytes 110600 | tf_op jit(solution)/shard_map/ppermute | solution.py:39
  41.2 0.0 collective-permute-done
  41.2 14.8 %collective-permute-done.1 = bf16[144,128]{1,0:T(8,128)(2,1)S(1)} collective-permute-done((bf16[144,128]{1,0:T(8,128)(2,1)S(1)}, bf16[144,128]{1,0:T(8,128)(2,1)S(1)}, u32[]{:S(2)}, u32[]{:S(2)}) %collective-permute-start.1) | collective-permute-done | bytes 36896 | tf_op jit(solution)/shard_map/ppermute | solution.py:39
  56.0 12.3 %all_gather.6.refs_0_ = bf16[8,144,128]{2,1,0:T(8,128)(2,1)S(1)} all-gather(bf16[2,144,128]{2,1,0:T(8,128)(2,1)S(1)} %pad_maximum_fusion), channel_id=1, replica_groups=mesh['pair'=8,'parity'=2,'core'=2,'y'=4,'x'=4] {'x'}, dimensions={0}, use_global_device_ids=true | all-gather | bytes 368640 | tf_op jit(solution)/shard_map/all_gather | solution.py:157
  68.3 1.9 %collective-permute-start.4 = (bf16[8,144,128]{2,1,0:T(8,128)(2,1)S(1)}, bf16[8,144,128]{2,1,0:T(8,128)(2,1)S(1)}, u32[]{:S(2)}, u32[]{:S(2)}) collective-permute-start(bf16[8,144,128]{2,1,0:T(8,128)(2,1)S(1)} %all_gather.6.refs_0_), channel_id=1, source_target_pairs={{0,12},{4,8},{8,4},{12,0},{1,13},{5,9},{9,5},{13,1},{2,14},{6,10},... | collective-permute-start | bytes 884744 | tf_op jit(solution)/shard_map/ppermute | solution.py:29
  70.2 3.8 %collective-permute-start.3 = (bf16[8,144,128]{2,1,0:T(8,128)(2,1)S(1)}, bf16[8,144,128]{2,1,0:T(8,128)(2,1)S(1)}, u32[]{:S(2)}, u32[]{:S(2)}) collective-permute-start(bf16[8,144,128]{2,1,0:T(8,128)(2,1)S(1)} %all_gather.6.refs_0_), channel_id=1, source_target_pairs={{0,8},{4,12},{8,0},{12,4},{1,9},{5,13},{9,1},{13,5},{2,10},{6,14},... | collective-permute-start | bytes 884744 | tf_op jit(solution)/shard_map/ppermute | solution.py:29
  74.0 4.1 %collective-permute-start.2 = (bf16[8,144,128]{2,1,0:T(8,128)(2,1)S(1)}, bf16[8,144,128]{2,1,0:T(8,128)(2,1)S(1)}, u32[]{:S(2)}, u32[]{:S(2)}) collective-permute-start(bf16[8,144,128]{2,1,0:T(8,128)(2,1)S(1)} %all_gather.6.refs_0_), channel_id=1, source_target_pairs={{0,4},{4,0},{8,12},{12,8},{1,5},{5,1},{9,13},{13,9},{2,6},{6,2},{1... | collective-permute-start | bytes 884744 | tf_op jit(solution)/shard_map/ppermute | solution.py:29
  78.2 4.1 %collective-permute-done.4.refs_3_ = bf16[8,144,128]{2,1,0:T(8,128)(2,1)S(1)} collective-permute-done((bf16[8,144,128]{2,1,0:T(8,128)(2,1)S(1)}, bf16[8,144,128]{2,1,0:T(8,128)(2,1)S(1)}, u32[]{:S(2)}, u32[]{:S(2)}) %collective-permute-start.4) | collective-permute-done | bytes 294944 | tf_op jit(solution)/shard_map/ppermute | solution.py:29
  82.3 7.6 %all-gather.2.cloned.1.call-done.refs_4_ = bf16[2048,1152]{1,0:T(8,128)(2,1)} async-done(((bf16[128,1152]{1,0:T(8,128)(2,1)}), bf16[2048,1152]{1,0:T(8,128)(2,1)}) %all-gather.2.cloned.1.call-update) | async-done | bytes 4718608 | tf_op jit(solution)/shard_map/all_gather | solution.py:138
  89.9 0.0 collective-permute-done.3.refs_2_
  89.9 0.0 collective-permute-done.2.refs_1_
  89.9 0.0 copy-start
  89.9 2.3 %copy-done = bf16[2048,1152]{1,0:T(8,128)(2,1)S(1)} copy-done((bf16[2048,1152]{1,0:T(8,128)(2,1)S(1)}, bf16[2048,1152]{1,0:T(8,128)(2,1)}, u32[]{:S(2)}) %copy-start) | copy-done | bytes 4718616
  92.3 0.0 copy-start.1
  92.3 2.1 %shard_map.70 = bf16[144,1152]{1,0:T(8,128)(2,1)S(1)} custom-call(s32[2,16]{1,0:T(2,128)S(1)} %get-tuple-element.12.place, bf16[8,144,128]{2,1,0:T(8,128)(2,1)S(1)} %all_gather.6.refs_0_, bf16[8,144,128]{2,1,0:T(8,128)(2,1)S(1)} %collective-permute-done.2.refs_1_, bf16[8,144,128]{2,1,0:T(8,128)(2,1)S(1)} %collective-permute-done.3.refs_2_, ...), custom_call_target="tpu_custom_call" | custom-call | flops 679477248 | bytes 5308416 | tf_op jit(solution)/shard_map/pallas_call | solution.py:120
  94.4 1.9 %collective-permute-start.5 = (bf16[144,1152]{1,0:T(8,128)(2,1)S(1)}, bf16[144,1152]{1,0:T(8,128)(2,1)S(1)}, u32[]{:S(2)}, u32[]{:S(2)}) collective-permute-start(bf16[144,1152]{1,0:T(8,128)(2,1)S(1)} %shard_map.70), channel_id=1, source_target_pairs={{0,32},{16,496},{32,64},{48,16},{64,96},{80,48},{96,128},{112,80},... | collective-permute-start | bytes 995336 | tf_op jit(solution)/shard_map/ppermute | solution.py:44
  96.3 0.6 fusion.1
  97.0 0.0 copy-done.2
  97.0 0.0 copy-done.1
  97.0 2.1 %shard_map.69 = f32[144,1152]{1,0:T(8,128)S(1)} custom-call(s32[2,16]{1,0:T(2,128)S(1)} %get-tuple-element.13.place, bf16[8,144,128]{2,1,0:T(8,128)(2,1)S(1)} %all_gather.6.refs_0_, bf16[8,144,128]{2,1,0:T(8,128)(2,1)S(1)} %collective-permute-done.2.refs_1_, bf16[8,144,128]{2,1,0:T(8,128)(2,1)S(1)} %collective-permute-done.3.refs_2_, ...), custom_call_target="tpu_custom_call" | custom-call | flops 679477248 | bytes 5308416 | tf_op jit(solution)/shard_map/pallas_call | solution.py:120
  99.1 5.5 %collective-permute-done.5 = bf16[144,1152]{1,0:T(8,128)(2,1)S(1)} collective-permute-done((bf16[144,1152]{1,0:T(8,128)(2,1)S(1)}, bf16[144,1152]{1,0:T(8,128)(2,1)S(1)}, u32[]{:S(2)}, u32[]{:S(2)}) %collective-permute-start.5) | collective-permute-done | bytes 331808 | tf_op jit(solution)/shard_map/ppermute | solution.py:44
  104.6 0.8 add_convert_fusion
  (5 shorter events, 0.1 us)
Async XLA Ops:
  7.2 89.8 %copy-start.2 = (bf16[144,1152]{1,0:T(8,128)(2,1)S(1)}, bf16[144,1152]{1,0:T(8,128)(2,1)}, u32[]{:S(2)}) copy-start(bf16[144,1152]{1,0:T(8,128)(2,1)} %refs_5_.1) | copy-start | bytes 995332
  7.2 82.8 %all-gather.2.cloned.1.call-start = ((), (), s32[]{:S(2)}) async-start(), calls=%async_computation | async-start | bytes 5013504 | tf_op jit(solution)/shard_map/all_gather | solution.py:138
  31.6 9.6 %collective-permute-start = (bf16[144,128]{1,0:T(8,128)(2,1)S(1)}, bf16[144,128]{1,0:T(8,128)(2,1)S(1)}, u32[]{:S(2)}, u32[]{:S(2)}) collective-permute-start(bf16[144,128]{1,0:T(8,128)(2,1)S(1)} %get-tuple-element.14), channel_id=1, source_target_pairs={{0,0},{1,65},{2,130},{3,195},{4,260},{5,325},{6,390},{7,455},{8,8}... | collective-permute-start | bytes 110600 | tf_op jit(solution)/shard_map/ppermute | solution.py:39
  39.3 16.7 %collective-permute-start.1 = (bf16[144,128]{1,0:T(8,128)(2,1)S(1)}, bf16[144,128]{1,0:T(8,128)(2,1)S(1)}, u32[]{:S(2)}, u32[]{:S(2)}) collective-permute-start(bf16[144,128]{1,0:T(8,128)(2,1)S(1)} %get-tuple-element.15), channel_id=1, source_target_pairs={{0,272},{1,337},{2,402},{3,467},{4,20},{5,85},{6,150},{7,215},{8,2... | collective-permute-start | bytes 110600 | tf_op jit(solution)/shard_map/ppermute | solution.py:39
  68.3 14.0 %collective-permute-start.4 = (bf16[8,144,128]{2,1,0:T(8,128)(2,1)S(1)}, bf16[8,144,128]{2,1,0:T(8,128)(2,1)S(1)}, u32[]{:S(2)}, u32[]{:S(2)}) collective-permute-start(bf16[8,144,128]{2,1,0:T(8,128)(2,1)S(1)} %all_gather.6.refs_0_), channel_id=1, source_target_pairs={{0,12},{4,8},{8,4},{12,0},{1,13},{5,9},{9,5},{13,1},{2,14},{6,10},... | collective-permute-start | bytes 884744 | tf_op jit(solution)/shard_map/ppermute | solution.py:29
  70.2 19.7 %collective-permute-start.3 = (bf16[8,144,128]{2,1,0:T(8,128)(2,1)S(1)}, bf16[8,144,128]{2,1,0:T(8,128)(2,1)S(1)}, u32[]{:S(2)}, u32[]{:S(2)}) collective-permute-start(bf16[8,144,128]{2,1,0:T(8,128)(2,1)S(1)} %all_gather.6.refs_0_), channel_id=1, source_target_pairs={{0,8},{4,12},{8,0},{12,4},{1,9},{5,13},{9,1},{13,5},{2,10},{6,14},... | collective-permute-start | bytes 884744 | tf_op jit(solution)/shard_map/ppermute | solution.py:29
  74.0 15.9 %collective-permute-start.2 = (bf16[8,144,128]{2,1,0:T(8,128)(2,1)S(1)}, bf16[8,144,128]{2,1,0:T(8,128)(2,1)S(1)}, u32[]{:S(2)}, u32[]{:S(2)}) collective-permute-start(bf16[8,144,128]{2,1,0:T(8,128)(2,1)S(1)} %all_gather.6.refs_0_), channel_id=1, source_target_pairs={{0,4},{4,0},{8,12},{12,8},{1,5},{5,1},{9,13},{13,9},{2,6},{6,2},{1... | collective-permute-start | bytes 884744 | tf_op jit(solution)/shard_map/ppermute | solution.py:29
  89.9 2.3 %copy-start = (bf16[2048,1152]{1,0:T(8,128)(2,1)S(1)}, bf16[2048,1152]{1,0:T(8,128)(2,1)}, u32[]{:S(2)}) copy-start(bf16[2048,1152]{1,0:T(8,128)(2,1)} %all-gather.2.cloned.1.call-done.refs_4_) | copy-start | bytes 14155780
  92.3 4.7 %copy-start.1 = (bf16[2048,1152]{1,0:T(8,128)(2,1)S(1)}, bf16[2048,1152]{1,0:T(8,128)(2,1)}, u32[]{:S(2)}) copy-start(bf16[2048,1152]{1,0:T(8,128)(2,1)} %all-gather.2.cloned.1.call-done.refs_4_) | copy-start | bytes 14155780
  94.4 10.2 %collective-permute-start.5 = (bf16[144,1152]{1,0:T(8,128)(2,1)S(1)}, bf16[144,1152]{1,0:T(8,128)(2,1)S(1)}, u32[]{:S(2)}, u32[]{:S(2)}) collective-permute-start(bf16[144,1152]{1,0:T(8,128)(2,1)S(1)} %shard_map.70), channel_id=1, source_target_pairs={{0,32},{16,496},{32,64},{48,16},{64,96},{80,48},{96,128},{112,80},... | collective-permute-start | bytes 995336 | tf_op jit(solution)/shard_map/ppermute | solution.py:44
Sparse Core Ops, SparseCore 0:
  10.1 79.7 all-gather.1

commit v4 on v3

--- a/solution.py
+++ b/solution.py
@@ -1,5 +1,3 @@
-import functools
-
 import jax
 import jax.numpy as jnp
 from jax import lax
@@ -97,37 +95,49 @@
     )(place, seg_rows, counts, hidden, grad_out)
 
 
-def product_kernel(own, place, *refs):
-    quarters, h_ref, rest = refs[:ROW], refs[ROW], refs[ROW + 1 :]
-    out_ref, w_ref = rest[-2], rest[-1]
-    for i in range(PLANES):
-        for k in range(ROW):
+def order_kernel(place, *refs):
+    quarters, out_refs = refs[:ROW], refs[ROW:]
+    for b in range(2):
+        for i in range(PLANES):
+            for k in range(ROW):
 
-            @pl.when(place[0, i] == k)
-            def _(i=i, k=k):
-                w_ref[:, i * SEQ : (i + 1) * SEQ] = quarters[k][place[1, i]]
-
-    summed = jnp.dot(w_ref[...], h_ref[...], preferred_element_type=jnp.float32)
-    if own:
-        summed += rest[0][...].astype(jnp.float32)
-    out_ref[...] = summed.astype(out_ref.dtype)
+                @pl.when(place[0, b * PLANES + i] == k)
+                def _(b=b, i=i, k=k):
+                    out_refs[b][:, i * SEQ : (i + 1) * SEQ] = quarters[k][place[1, b * PLANES + i]]
 
 
-def product(place, quarters, h_all, noise=None):
-    own = noise is not None
+def in_order(place, quarters):
+    vmem = pl.BlockSpec(memory_space=pltpu.VMEM)
+    return pl.pallas_call(
+        order_kernel,
+        in_specs=[pl.BlockSpec(memory_space=pltpu.SMEM)] + [vmem] * ROW,
+        out_specs=[vmem, vmem],
+        out_shape=[jax.ShapeDtypeStruct((ROWS, PLANES * SEQ), jnp.bfloat16)] * 2,
+        compiler_params=pltpu.CompilerParams(vmem_limit_bytes=24 * 1024 * 1024),
+    )(place, *quarters)
+
+
+def product_kernel(*refs):
+    w_ref, h_ref, *noise_ref = refs[:-1]
+    summed = jnp.dot(w_ref[...], h_ref[...], preferred_element_type=jnp.float32)
+    for ref in noise_ref:
+        summed += ref[...].astype(jnp.float32)
+    refs[-1][...] = summed.astype(refs[-1].dtype)
+
+
+def product(rows, h_all, *noise):
     tokens, columns = h_all.shape
     vmem = pl.BlockSpec(memory_space=pltpu.VMEM)
     return pl.pallas_call(
-        functools.partial(product_kernel, own),
-        in_specs=[pl.BlockSpec(memory_space=pltpu.SMEM)] + [vmem] * (ROW + 1 + own),
+        product_kernel,
+        in_specs=[vmem] * (2 + len(noise)),
         out_specs=vmem,
-        out_shape=jax.ShapeDtypeStruct((ROWS, columns), jnp.float32 if own else jnp.bfloat16),
-        scratch_shapes=[pltpu.VMEM((ROWS, tokens), jnp.bfloat16)],
+        out_shape=jax.ShapeDtypeStruct((ROWS, columns), jnp.float32 if noise else jnp.bfloat16),
         compiler_params=pltpu.CompilerParams(vmem_limit_bytes=24 * 1024 * 1024),
         cost_estimate=pl.CostEstimate(
             flops=2 * tokens * ROWS * columns, bytes_accessed=2 * tokens * (ROWS + columns), transcendentals=0
         ),
-    )(place, *quarters, h_all, *([noise] if own else []))
+    )(rows, h_all, *noise)
 
 
 def per_device(hidden, grad_out, seg_ids, seg_counts, added_noise):
@@ -156,7 +166,6 @@
     keep, swap = fan_out(weighted(keep), 0, False), fan_out(weighted(swap), 4, True)
     row = lax.all_gather(jnp.stack([keep, swap]), "x", axis=0, tiled=True)
     one, two, three = [along_y(row, k) for k in range(1, ROW)]
-    h_all, three = lax.optimization_barrier((h_all, three))
     quarters = [row, one, two, three]
 
     sequence = jnp.arange(PLANES)
@@ -164,11 +173,12 @@
     came = (pair - sequence // 2 + 2 * PAIRS - 4 * other) % PAIRS
     inside = came % ROW * 2 + other
 
-    def place(block):
-        return jnp.stack([(2 * block + came // ROW) ^ y, inside]).astype(jnp.int32)
-
-    handed = to_neighbour(product(place(1), quarters, h_all))
-    summed = product(place(0), quarters, h_all, added_noise)
+    quarter = jnp.concatenate([came // ROW, 2 + came // ROW]) ^ y
+    place = jnp.stack([quarter, jnp.tile(inside, 2)]).astype(jnp.int32)
+    own, neighbours = in_order(place, quarters)
+    own, neighbours, h_all = lax.optimization_barrier((own, neighbours, h_all))
+    handed = to_neighbour(product(neighbours, h_all))
+    summed = product(own, h_all, added_noise)
     weight_grad = (summed + handed.astype(jnp.float32)).astype(jnp.bfloat16)
     return (weight_grad, norms)
 

time: 113 us -> 112 us (level)
  the two profiles are of different devices: /device:TPU:30 before, /device:TPU:1 now
where the time goes in v4:
time: 112 us; the launch traced here: 111 us
  starting transfers between devices  35.8 us (32%)
  blocking collectives  29 us (26%)
  waiting for transfers between devices  20 us (18%)
  between operations  14.2 us (13%)
  Pallas kernels  6.53 us (6%)
  other arithmetic  3.04 us (3%)
  local copies, waits for them, and re-layouts  2.42 us (2%)
    ppermute x2, starting transfers between devices, fan_out(): return lax.ppermute(value, ('pair', 'parity', 'core', 'y', 'x'), perm)  20.7 us
    psum x2, blocking collectives, per_device(): squares = lax.psum(lax.psum(squares, 'x'), 'y')  18.3 us
    ppermute x3, waiting for transfers between devices, along_y(): return lax.ppermute(value, 'y', [(i, i ^ distance) for i in range(ROW)])  10.7 us
    all_gather x1, blocking collectives, per_device(): row = lax.all_gather(jnp.stack([keep, swap]), 'x', axis=0, tiled=True)  10.6 us
    ppermute x3, starting transfers between devices, along_y(): return lax.ppermute(value, 'y', [(i, i ^ distance) for i in range(ROW)])  9.57 us
    ppermute x2, waiting for transfers between devices, fan_out(): return lax.ppermute(value, ('pair', 'parity', 'core', 'y', 'x'), perm)  5.74 us
    ppermute x1, starting transfers between devices, to_neighbour(): return lax.ppermute(value, ('pair', 'parity', 'core'), perm)  5.47 us
    ppermute x1, waiting for transfers between devices, to_neighbour(): return lax.ppermute(value, ('pair', 'parity', 'core'), perm)  2.91 us
  transfers between devices with their start and end apart: 7, of which 4 were waited for; matrix products, arithmetic and copies ran while one was open for 2% of the time, Pallas kernels for 5%

profile of v4, /device:TPU:1, one launch (start us, length us, event | category | flops | bytes accessed | tf_op | source)
XLA Modules:
  0.0 111.0 jit_solution(2768949950517380230)
XLA Ops:
  7.2 0.0 copy-start.1
  7.2 0.0 all-gather.2.cloned.1.call-start
  7.2 0.7 all-gather.2.cloned.1.call-update
  8.0 0.6 pad_add_fusion.1.place
  8.6 2.8 %shard_map.68 = (f32[16,128]{1,0:T(8,128)}, bf16[144,128]{1,0:T(8,128)(2,1)}, bf16[144,128]{1,0:T(8,128)(2,1)}) custom-call(s32[3]{0:T(128)} %pad_add_fusion.1.place, s32[32,128]{1,0:T(8,128)} %bitcast.14, s32[8]{0:T(128)} %count_ref.1, bf16[128,1152]{1,0:T(8,128)(2,1)} %hidden_ref.1, bf16[128,4608]{1,0:T(8,128)(2,1)} %grad_ref.1), custom_call_target="tpu_custom_call" | custom-call | tf_op jit(solution)/shard_map/pallas_call | solution.py:88
  11.4 9.5 %psum.14 = f32[16,128]{1,0:T(8,128)S(1)} all-reduce(f32[16,128]{1,0:T(8,128)} %get-tuple-element.11), channel_id=1, replica_groups=mesh['pair'=8,'parity'=2,'core'=2,'y'=4,'x'=4] {'x'}, use_global_device_ids=true, to_apply=%region_0.1 | all-reduce | flops 2048 | bytes 16384 | tf_op jit(solution)/shard_map/psum | solution.py:159
  20.9 8.8 %psum.15 = f32[16,128]{1,0:T(8,128)S(1)} all-reduce(f32[16,128]{1,0:T(8,128)S(1)} %psum.14), channel_id=1, replica_groups=mesh['pair'=8,'parity'=2,'core'=2,'y'=4,'x'=4] {'y'}, use_global_device_ids=true, to_apply=%region_1.2 | all-reduce | flops 2048 | bytes 16384 | tf_op jit(solution)/shard_map/psum | solution.py:159
  29.8 0.8 multiply_convert_fusion.1
  30.6 0.7 collective-permute-start
  31.3 20.0 %collective-permute-start.1 = (bf16[144,128]{1,0:T(8,128)(2,1)S(1)}, bf16[144,128]{1,0:T(8,128)(2,1)S(1)}, u32[]{:S(2)}, u32[]{:S(2)}) collective-permute-start(bf16[144,128]{1,0:T(8,128)(2,1)S(1)} %get-tuple-element.19), channel_id=1, source_target_pairs={{0,272},{1,337},{2,402},{3,467},{4,20},{5,85},{6,150},{7,215},{8,2... | collective-permute-start | bytes 110600 | tf_op jit(solution)/shard_map/ppermute | solution.py:37
  51.4 0.1 stack_tile.3
  51.4 0.0 collective-permute-done
  51.4 5.7 %collective-permute-done.1 = bf16[144,128]{1,0:T(8,128)(2,1)S(1)} collective-permute-done((bf16[144,128]{1,0:T(8,128)(2,1)S(1)}, bf16[144,128]{1,0:T(8,128)(2,1)S(1)}, u32[]{:S(2)}, u32[]{:S(2)}) %collective-permute-start.1) | collective-permute-done | bytes 36896 | tf_op jit(solution)/shard_map/ppermute | solution.py:37
  57.2 10.6 %all_gather.6.refs_0_ = bf16[8,144,128]{2,1,0:T(8,128)(2,1)S(1)} all-gather(bf16[2,144,128]{2,1,0:T(8,128)(2,1)S(1)} %pad_maximum_fusion), channel_id=1, replica_groups=mesh['pair'=8,'parity'=2,'core'=2,'y'=4,'x'=4] {'x'}, dimensions={0}, use_global_device_ids=true | all-gather | bytes 368640 | tf_op jit(solution)/shard_map/all_gather | solution.py:167
  67.8 2.5 %collective-permute-start.2 = (bf16[8,144,128]{2,1,0:T(8,128)(2,1)S(1)}, bf16[8,144,128]{2,1,0:T(8,128)(2,1)S(1)}, u32[]{:S(2)}, u32[]{:S(2)}) collective-permute-start(bf16[8,144,128]{2,1,0:T(8,128)(2,1)S(1)} %all_gather.6.refs_0_), channel_id=1, source_target_pairs={{0,4},{4,0},{8,12},{12,8},{1,5},{5,1},{9,13},{13,9},{2,6},{6,2},{1... | collective-permute-start | bytes 884744 | tf_op jit(solution)/shard_map/ppermute | solution.py:27
  70.4 1.9 %collective-permute-start.3 = (bf16[8,144,128]{2,1,0:T(8,128)(2,1)S(1)}, bf16[8,144,128]{2,1,0:T(8,128)(2,1)S(1)}, u32[]{:S(2)}, u32[]{:S(2)}) collective-permute-start(bf16[8,144,128]{2,1,0:T(8,128)(2,1)S(1)} %all_gather.6.refs_0_), channel_id=1, source_target_pairs={{0,8},{4,12},{8,0},{12,4},{1,9},{5,13},{9,1},{13,5},{2,10},{6,14},... | collective-permute-start | bytes 884744 | tf_op jit(solution)/shard_map/ppermute | solution.py:27
  72.3 5.1 %collective-permute-start.4 = (bf16[8,144,128]{2,1,0:T(8,128)(2,1)S(1)}, bf16[8,144,128]{2,1,0:T(8,128)(2,1)S(1)}, u32[]{:S(2)}, u32[]{:S(2)}) collective-permute-start(bf16[8,144,128]{2,1,0:T(8,128)(2,1)S(1)} %all_gather.6.refs_0_), channel_id=1, source_target_pairs={{0,12},{4,8},{8,4},{12,0},{1,13},{5,9},{9,5},{13,1},{2,14},{6,10},... | collective-permute-start | bytes 884744 | tf_op jit(solution)/shard_map/ppermute | solution.py:27
  77.5 0.1 add_xor_fusion
  77.5 0.0 collective-permute-done.2.refs_1_
  77.5 4.6 %collective-permute-done.3.refs_2_ = bf16[8,144,128]{2,1,0:T(8,128)(2,1)S(1)} collective-permute-done((bf16[8,144,128]{2,1,0:T(8,128)(2,1)S(1)}, bf16[8,144,128]{2,1,0:T(8,128)(2,1)S(1)}, u32[]{:S(2)}, u32[]{:S(2)}) %collective-permute-start.3) | collective-permute-done | bytes 294944 | tf_op jit(solution)/shard_map/ppermute | solution.py:27
  82.1 6.1 %collective-permute-done.4.refs_3_ = bf16[8,144,128]{2,1,0:T(8,128)(2,1)S(1)} collective-permute-done((bf16[8,144,128]{2,1,0:T(8,128)(2,1)S(1)}, bf16[8,144,128]{2,1,0:T(8,128)(2,1)S(1)}, u32[]{:S(2)}, u32[]{:S(2)}) %collective-permute-start.4) | collective-permute-done | bytes 294944 | tf_op jit(solution)/shard_map/ppermute | solution.py:27
  88.2 1.9 %shard_map.69 = (bf16[144,2048]{1,0:T(8,128)(2,1)S(1)}, bf16[144,2048]{1,0:T(8,128)(2,1)S(1)}) custom-call(s32[2,32]{1,0:T(2,128)S(1)} %pad_add_fusion.place, bf16[8,144,128]{2,1,0:T(8,128)(2,1)S(1)} %all_gather.6.refs_0_, bf16[8,144,128]{2,1,0:T(8,128)(2,1)S(1)} %collective-permute-done.2.refs_1_, bf16[8,144,128]{2,1,0:T(8,128)(2,1)S(1)} %collective-permute-done.3.refs_2_, ...), custom_call_target="tpu_custom_call" | custom-call | tf_op jit(solution)/shard_map/pallas_call | solution.py:111
  90.1 0.0 all-gather.2.cloned.1.call-done.refs_1_
  90.1 0.0 copy-start
  90.1 2.3 %copy-done = bf16[2048,1152]{1,0:T(8,128)(2,1)S(1)} copy-done((bf16[2048,1152]{1,0:T(8,128)(2,1)S(1)}, bf16[2048,1152]{1,0:T(8,128)(2,1)}, u32[]{:S(2)}) %copy-start) | copy-done | bytes 4718616
  92.4 0.9 shard_map.71
  93.4 5.5 %collective-permute-start.5 = (bf16[144,1152]{1,0:T(8,128)(2,1)S(1)}, bf16[144,1152]{1,0:T(8,128)(2,1)S(1)}, u32[]{:S(2)}, u32[]{:S(2)}) collective-permute-start(bf16[144,1152]{1,0:T(8,128)(2,1)S(1)} %shard_map.71), channel_id=1, source_target_pairs={{0,32},{16,496},{32,64},{48,16},{64,96},{80,48},{96,128},{112,80},... | collective-permute-start | bytes 995336 | tf_op jit(solution)/shard_map/ppermute | solution.py:42
  98.9 0.6 fusion.1
  99.5 0.0 copy-done.1
  99.5 0.9 shard_map.70
  100.4 2.9 %collective-permute-done.5 = bf16[144,1152]{1,0:T(8,128)(2,1)S(1)} collective-permute-done((bf16[144,1152]{1,0:T(8,128)(2,1)S(1)}, bf16[144,1152]{1,0:T(8,128)(2,1)S(1)}, u32[]{:S(2)}, u32[]{:S(2)}) %collective-permute-start.5) | collective-permute-done | bytes 331808 | tf_op jit(solution)/shard_map/ppermute | solution.py:42
  103.4 0.8 add_convert_fusion
  (6 shorter events, 0.1 us)
Async XLA Ops:
  7.2 92.3 %copy-start.1 = (bf16[144,1152]{1,0:T(8,128)(2,1)S(1)}, bf16[144,1152]{1,0:T(8,128)(2,1)}, u32[]{:S(2)}) copy-start(bf16[144,1152]{1,0:T(8,128)(2,1)} %refs_2_.1) | copy-start | bytes 995332
  7.2 82.9 %all-gather.2.cloned.1.call-start = ((), (), s32[]{:S(2)}) async-start(), calls=%async_computation | async-start | bytes 5013504 | tf_op jit(solution)/shard_map/all_gather | solution.py:148
  30.6 20.8 %collective-permute-start = (bf16[144,128]{1,0:T(8,128)(2,1)S(1)}, bf16[144,128]{1,0:T(8,128)(2,1)S(1)}, u32[]{:S(2)}, u32[]{:S(2)}) collective-permute-start(bf16[144,128]{1,0:T(8,128)(2,1)S(1)} %get-tuple-element.18), channel_id=1, source_target_pairs={{0,0},{1,65},{2,130},{3,195},{4,260},{5,325},{6,390},{7,455},{8,8}... | collective-permute-start | bytes 110600 | tf_op jit(solution)/shard_map/ppermute | solution.py:37
  31.3 25.9 %collective-permute-start.1 = (bf16[144,128]{1,0:T(8,128)(2,1)S(1)}, bf16[144,128]{1,0:T(8,128)(2,1)S(1)}, u32[]{:S(2)}, u32[]{:S(2)}) collective-permute-start(bf16[144,128]{1,0:T(8,128)(2,1)S(1)} %get-tuple-element.19), channel_id=1, source_target_pairs={{0,272},{1,337},{2,402},{3,467},{4,20},{5,85},{6,150},{7,215},{8,2... | collective-permute-start | bytes 110600 | tf_op jit(solution)/shard_map/ppermute | solution.py:37
  67.8 9.7 %collective-permute-start.2 = (bf16[8,144,128]{2,1,0:T(8,128)(2,1)S(1)}, bf16[8,144,128]{2,1,0:T(8,128)(2,1)S(1)}, u32[]{:S(2)}, u32[]{:S(2)}) collective-permute-start(bf16[8,144,128]{2,1,0:T(8,128)(2,1)S(1)} %all_gather.6.refs_0_), channel_id=1, source_target_pairs={{0,4},{4,0},{8,12},{12,8},{1,5},{5,1},{9,13},{13,9},{2,6},{6,2},{1... | collective-permute-start | bytes 884744 | tf_op jit(solution)/shard_map/ppermute | solution.py:27
  70.4 11.8 %collective-permute-start.3 = (bf16[8,144,128]{2,1,0:T(8,128)(2,1)S(1)}, bf16[8,144,128]{2,1,0:T(8,128)(2,1)S(1)}, u32[]{:S(2)}, u32[]{:S(2)}) collective-permute-start(bf16[8,144,128]{2,1,0:T(8,128)(2,1)S(1)} %all_gather.6.refs_0_), channel_id=1, source_target_pairs={{0,8},{4,12},{8,0},{12,4},{1,9},{5,13},{9,1},{13,5},{2,10},{6,14},... | collective-permute-start | bytes 884744 | tf_op jit(solution)/shard_map/ppermute | solution.py:27
  72.3 15.9 %collective-permute-start.4 = (bf16[8,144,128]{2,1,0:T(8,128)(2,1)S(1)}, bf16[8,144,128]{2,1,0:T(8,128)(2,1)S(1)}, u32[]{:S(2)}, u32[]{:S(2)}) collective-permute-start(bf16[8,144,128]{2,1,0:T(8,128)(2,1)S(1)} %all_gather.6.refs_0_), channel_id=1, source_target_pairs={{0,12},{4,8},{8,4},{12,0},{1,13},{5,9},{9,5},{13,1},{2,14},{6,10},... | collective-permute-start | bytes 884744 | tf_op jit(solution)/shard_map/ppermute | solution.py:27
  90.1 2.3 %copy-start = (bf16[2048,1152]{1,0:T(8,128)(2,1)S(1)}, bf16[2048,1152]{1,0:T(8,128)(2,1)}, u32[]{:S(2)}) copy-start(bf16[2048,1152]{1,0:T(8,128)(2,1)} %all-gather.2.cloned.1.call-done.refs_1_) | copy-start | bytes 14155780
  93.4 10.0 %collective-permute-start.5 = (bf16[144,1152]{1,0:T(8,128)(2,1)S(1)}, bf16[144,1152]{1,0:T(8,128)(2,1)S(1)}, u32[]{:S(2)}, u32[]{:S(2)}) collective-permute-start(bf16[144,1152]{1,0:T(8,128)(2,1)S(1)} %shard_map.71), channel_id=1, source_target_pairs={{0,32},{16,496},{32,64},{48,16},{64,96},{80,48},{96,128},{112,80},... | collective-permute-start | bytes 995336 | tf_op jit(solution)/shard_map/ppermute | solution.py:42
Sparse Core Ops, SparseCore 0:
  10.1 79.5 all-gather.1

commit v5 on v4

--- a/solution.py
+++ b/solution.py
@@ -42,8 +42,21 @@
     return lax.ppermute(value, ("pair", "parity", "core"), perm)
 
 
-def squares_kernel(place, seg_ref, count_ref, hidden_ref, grad_ref, out_ref, keep_ref, swap_ref, turned_ref):
-    seg = seg_ref[pl.ds(place[0], 1), :]
+def block_starts():
+    plane, core = lax.axis_index("pair") * 2 + lax.axis_index("parity"), lax.axis_index("core")
+    x, y = lax.axis_index("x"), lax.axis_index("y")
+    ahead = plane + 2 * ((y * ROW + x) % PAIRS)
+
+    def start(to_plane, of_core):
+        shift = jnp.where(y < 2, 0, 1 - 2 * of_core)
+        return ((to_plane + shift + PLANES) % PLANES * 2 + of_core) * ROWS
+
+    return plane * 2 + core, (start(ahead, core), start(ahead + 8, 1 - core))
+
+
+def squares_kernel(seg_ref, count_ref, hidden_ref, grad_ref, out_ref, keep_ref, swap_ref, turned_ref):
+    dp, starts = block_starts()
+    seg = seg_ref[pl.ds(dp, 1), :]
     row = lax.broadcasted_iota(jnp.int32, (SEQ, SEQ), 0)
     column = lax.broadcasted_iota(jnp.int32, (SEQ, SEQ), 1)
     count = jnp.zeros((1, SEQ), jnp.float32)
@@ -75,24 +88,24 @@
 
     window = turned_ref.shape[0]
     for n, piece_ref in enumerate((keep_ref, swap_ref)):
-        start = place[1 + n]
+        start = starts[n]
         at = pl.multiple_of(jnp.minimum(start // SEQ * SEQ, D - window), SEQ)
         turned_ref[...] = scaled(grad_ref[:, pl.ds(at, window)]).astype(jnp.float32).T
         inside = pl.multiple_of(start - at, 16)
         piece_ref[...] = turned_ref[pl.ds(inside, ROWS), :].astype(jnp.bfloat16)
 
 
-def partial_squares(place, seg_rows, counts, hidden, grad_out):
+def partial_squares(seg_rows, counts, hidden, grad_out):
     vmem, smem = pl.BlockSpec(memory_space=pltpu.VMEM), pl.BlockSpec(memory_space=pltpu.SMEM)
     piece = jax.ShapeDtypeStruct((ROWS, SEQ), jnp.bfloat16)
     return pl.pallas_call(
         squares_kernel,
-        in_specs=[smem, vmem, smem, vmem, vmem],
+        in_specs=[vmem, smem, vmem, vmem],
         out_specs=[vmem] * 3,
         out_shape=[jax.ShapeDtypeStruct((2 * NSEG, SEQ), jnp.float32), piece, piece],
         scratch_shapes=[pltpu.VMEM((3 * SEQ, SEQ), jnp.float32)],
         compiler_params=pltpu.CompilerParams(vmem_limit_bytes=56 * 1024 * 1024),
-    )(place, seg_rows, counts, hidden, grad_out)
+    )(seg_rows, counts, hidden, grad_out)
 
 
 def order_kernel(place, *refs):
@@ -149,13 +162,7 @@
 
     seg_rows = seg_ids.reshape(-1, SEQ)
 
-    def start(to_plane, of_core):
-        shift = jnp.where(y < 2, 0, 1 - 2 * of_core)
-        return ((to_plane + shift + PLANES) % PLANES * 2 + of_core) * ROWS
-
-    ahead = plane + 2 * (j % PAIRS)
-    here = jnp.stack([dp, start(ahead, core), start(ahead + 8, 1 - core)]).astype(jnp.int32)
-    squares, keep, swap = partial_squares(here, seg_rows, seg_counts, hidden, grad_out)
+    squares, keep, swap = partial_squares(seg_rows, seg_counts, hidden, grad_out)
     squares = lax.psum(lax.psum(squares, "x"), "y")
     norms = jnp.sqrt(squares[:NSEG, 0] + EPSILON)
     factor = jnp.minimum(1.0, clip_bound() / jnp.sqrt(squares[NSEG : NSEG + 1] + EPSILON))

time: 112 us -> 111 us (level)
  waiting for transfers between devices: 20 us -> 18.2 us
  starting transfers between devices: 35.8 us -> 37.4 us
    ppermute x1, starting transfers between devices: 5.47 us -> 7.13 us  [to_neighbour(): return lax.ppermute(value, ('pair', 'parity', 'core'), perm)]
  transfers between devices with their start and end apart: 7 -> 7, of which waited for: 4 -> 5; matrix products, arithmetic and copies ran while one was open for 2% -> 2% of each run, Pallas kernels for 5% -> 5%
where the time goes in v5:
time: 111 us; the launch traced here: 110 us
  starting transfers between devices  37.4 us (34%)
  blocking collectives  29 us (26%)
  waiting for transfers between devices  18.2 us (16%)
  between operations  14.2 us (13%)
  Pallas kernels  6.56 us (6%)
  local copies, waits for them, and re-layouts  2.42 us (2%)
  other arithmetic  2.39 us (2%)
    ppermute x2, starting transfers between devices, fan_out(): return lax.ppermute(value, ('pair', 'parity', 'core', 'y', 'x'), perm)  20.7 us
    psum x2, blocking collectives, per_device(): squares = lax.psum(lax.psum(squares, 'x'), 'y')  18.3 us
    all_gather x1, blocking collectives, per_device(): row = lax.all_gather(jnp.stack([keep, swap]), 'x', axis=0, tiled=True)  10.6 us
    ppermute x3, waiting for transfers between devices, along_y(): return lax.ppermute(value, 'y', [(i, i ^ distance) for i in range(ROW)])  9.73 us
    ppermute x3, starting transfers between devices, along_y(): return lax.ppermute(value, 'y', [(i, i ^ distance) for i in range(ROW)])  9.57 us
    ppermute x1, starting transfers between devices, to_neighbour(): return lax.ppermute(value, ('pair', 'parity', 'core'), perm)  7.13 us
    ppermute x2, waiting for transfers between devices, fan_out(): return lax.ppermute(value, ('pair', 'parity', 'core', 'y', 'x'), perm)  5.03 us
    pallas_call x1, Pallas kernels, partial_squares(): pl.pallas_call(squares_kernel, in_specs=[vmem, smem, vmem, vmem], out_spe...  2.82 us
  transfers between devices with their start and end apart: 7, of which 5 were waited for; matrix products, arithmetic and copies ran while one was open for 2% of the time, Pallas kernels for 5%

profile of v5, /device:TPU:1, one launch (start us, length us, event | category | flops | bytes accessed | tf_op | source)
XLA Modules:
  0.0 110.2 jit_solution(18125141947131591839)
XLA Ops:
  7.2 0.0 copy-start.1
  7.2 0.0 all-gather.2.cloned.1.call-start
  7.2 0.7 all-gather.2.cloned.1.call-update
  7.9 2.8 %shard_map.68 = (f32[16,128]{1,0:T(8,128)}, bf16[144,128]{1,0:T(8,128)(2,1)}, bf16[144,128]{1,0:T(8,128)(2,1)}) custom-call(s32[32,128]{1,0:T(8,128)} %bitcast.11, s32[8]{0:T(128)} %count_ref.1, bf16[128,1152]{1,0:T(8,128)(2,1)} %hidden_ref.1, bf16[128,4608]{1,0:T(8,128)(2,1)} %grad_ref.1), custom_call_target="tpu_custom_call" | custom-call | tf_op jit(solution)/shard_map/pallas_call | solution.py:101
  10.7 9.5 %psum.14 = f32[16,128]{1,0:T(8,128)S(1)} all-reduce(f32[16,128]{1,0:T(8,128)} %get-tuple-element.11), channel_id=1, replica_groups=mesh['pair'=8,'parity'=2,'core'=2,'y'=4,'x'=4] {'x'}, use_global_device_ids=true, to_apply=%region_0.0 | all-reduce | flops 2048 | bytes 16384 | tf_op jit(solution)/shard_map/psum | solution.py:166
  20.2 8.8 %psum.15 = f32[16,128]{1,0:T(8,128)S(1)} all-reduce(f32[16,128]{1,0:T(8,128)S(1)} %psum.14), channel_id=1, replica_groups=mesh['pair'=8,'parity'=2,'core'=2,'y'=4,'x'=4] {'y'}, use_global_device_ids=true, to_apply=%region_1.0 | all-reduce | flops 2048 | bytes 16384 | tf_op jit(solution)/shard_map/psum | solution.py:166
  29.1 0.8 multiply_convert_fusion.1
  29.9 0.7 collective-permute-start
  30.6 20.0 %collective-permute-start.1 = (bf16[144,128]{1,0:T(8,128)(2,1)S(1)}, bf16[144,128]{1,0:T(8,128)(2,1)S(1)}, u32[]{:S(2)}, u32[]{:S(2)}) collective-permute-start(bf16[144,128]{1,0:T(8,128)(2,1)S(1)} %get-tuple-element.19), channel_id=1, source_target_pairs={{0,272},{1,337},{2,402},{3,467},{4,20},{5,85},{6,150},{7,215},{8,2... | collective-permute-start | bytes 110600 | tf_op jit(solution)/shard_map/ppermute | solution.py:37
  50.7 0.1 stack_tile.3
  50.8 0.0 collective-permute-done
  50.8 5.0 %collective-permute-done.1 = bf16[144,128]{1,0:T(8,128)(2,1)S(1)} collective-permute-done((bf16[144,128]{1,0:T(8,128)(2,1)S(1)}, bf16[144,128]{1,0:T(8,128)(2,1)S(1)}, u32[]{:S(2)}, u32[]{:S(2)}) %collective-permute-start.1) | collective-permute-done | bytes 36896 | tf_op jit(solution)/shard_map/ppermute | solution.py:37
  55.8 10.6 %all_gather.6.refs_0_ = bf16[8,144,128]{2,1,0:T(8,128)(2,1)S(1)} all-gather(bf16[2,144,128]{2,1,0:T(8,128)(2,1)S(1)} %pad_maximum_fusion), channel_id=1, replica_groups=mesh['pair'=8,'parity'=2,'core'=2,'y'=4,'x'=4] {'x'}, dimensions={0}, use_global_device_ids=true | all-gather | bytes 368640 | tf_op jit(solution)/shard_map/all_gather | solution.py:174
  66.4 1.9 %collective-permute-start.2 = (bf16[8,144,128]{2,1,0:T(8,128)(2,1)S(1)}, bf16[8,144,128]{2,1,0:T(8,128)(2,1)S(1)}, u32[]{:S(2)}, u32[]{:S(2)}) collective-permute-start(bf16[8,144,128]{2,1,0:T(8,128)(2,1)S(1)} %all_gather.6.refs_0_), channel_id=1, source_target_pairs={{0,4},{4,0},{8,12},{12,8},{1,5},{5,1},{9,13},{13,9},{2,6},{6,2},{1... | collective-permute-start | bytes 884744 | tf_op jit(solution)/shard_map/ppermute | solution.py:27
  68.4 2.4 %collective-permute-start.3 = (bf16[8,144,128]{2,1,0:T(8,128)(2,1)S(1)}, bf16[8,144,128]{2,1,0:T(8,128)(2,1)S(1)}, u32[]{:S(2)}, u32[]{:S(2)}) collective-permute-start(bf16[8,144,128]{2,1,0:T(8,128)(2,1)S(1)} %all_gather.6.refs_0_), channel_id=1, source_target_pairs={{0,8},{4,12},{8,0},{12,4},{1,9},{5,13},{9,1},{13,5},{2,10},{6,14},... | collective-permute-start | bytes 884744 | tf_op jit(solution)/shard_map/ppermute | solution.py:27
  70.7 5.3 %collective-permute-start.4 = (bf16[8,144,128]{2,1,0:T(8,128)(2,1)S(1)}, bf16[8,144,128]{2,1,0:T(8,128)(2,1)S(1)}, u32[]{:S(2)}, u32[]{:S(2)}) collective-permute-start(bf16[8,144,128]{2,1,0:T(8,128)(2,1)S(1)} %all_gather.6.refs_0_), channel_id=1, source_target_pairs={{0,12},{4,8},{8,4},{12,0},{1,13},{5,9},{9,5},{13,1},{2,14},{6,10},... | collective-permute-start | bytes 884744 | tf_op jit(solution)/shard_map/ppermute | solution.py:27
  76.1 0.1 add_xor_fusion
  76.2 0.0 collective-permute-done.2.refs_1_
  76.2 3.9 %collective-permute-done.3.refs_2_ = bf16[8,144,128]{2,1,0:T(8,128)(2,1)S(1)} collective-permute-done((bf16[8,144,128]{2,1,0:T(8,128)(2,1)S(1)}, bf16[8,144,128]{2,1,0:T(8,128)(2,1)S(1)}, u32[]{:S(2)}, u32[]{:S(2)}) %collective-permute-start.3) | collective-permute-done | bytes 294944 | tf_op jit(solution)/shard_map/ppermute | solution.py:27
  80.0 5.8 %collective-permute-done.4.refs_3_ = bf16[8,144,128]{2,1,0:T(8,128)(2,1)S(1)} collective-permute-done((bf16[8,144,128]{2,1,0:T(8,128)(2,1)S(1)}, bf16[8,144,128]{2,1,0:T(8,128)(2,1)S(1)}, u32[]{:S(2)}, u32[]{:S(2)}) %collective-permute-start.4) | collective-permute-done | bytes 294944 | tf_op jit(solution)/shard_map/ppermute | solution.py:27
  85.9 1.9 %shard_map.69 = (bf16[144,2048]{1,0:T(8,128)(2,1)S(1)}, bf16[144,2048]{1,0:T(8,128)(2,1)S(1)}) custom-call(s32[2,32]{1,0:T(2,128)S(1)} %pad_add_fusion.place, bf16[8,144,128]{2,1,0:T(8,128)(2,1)S(1)} %all_gather.6.refs_0_, bf16[8,144,128]{2,1,0:T(8,128)(2,1)S(1)} %collective-permute-done.2.refs_1_, bf16[8,144,128]{2,1,0:T(8,128)(2,1)S(1)} %collective-permute-done.3.refs_2_, ...), custom_call_target="tpu_custom_call" | custom-call | tf_op jit(solution)/shard_map/pallas_call | solution.py:124
  87.8 0.3 all-gather.2.cloned.1.call-done.refs_1_
  88.0 0.0 copy-start
  88.0 2.3 %copy-done = bf16[2048,1152]{1,0:T(8,128)(2,1)S(1)} copy-done((bf16[2048,1152]{1,0:T(8,128)(2,1)S(1)}, bf16[2048,1152]{1,0:T(8,128)(2,1)}, u32[]{:S(2)}) %copy-start) | copy-done | bytes 4718616
  90.4 0.9 shard_map.71
  91.3 7.1 %collective-permute-start.5 = (bf16[144,1152]{1,0:T(8,128)(2,1)S(1)}, bf16[144,1152]{1,0:T(8,128)(2,1)S(1)}, u32[]{:S(2)}, u32[]{:S(2)}) collective-permute-start(bf16[144,1152]{1,0:T(8,128)(2,1)S(1)} %shard_map.71), channel_id=1, source_target_pairs={{0,32},{16,496},{32,64},{48,16},{64,96},{80,48},{96,128},{112,80},... | collective-permute-start | bytes 995336 | tf_op jit(solution)/shard_map/ppermute | solution.py:42
  98.5 0.6 fusion.1
  99.1 0.0 copy-done.1
  99.1 0.9 shard_map.70
  100.0 2.5 %collective-permute-done.5 = bf16[144,1152]{1,0:T(8,128)(2,1)S(1)} collective-permute-done((bf16[144,1152]{1,0:T(8,128)(2,1)S(1)}, bf16[144,1152]{1,0:T(8,128)(2,1)S(1)}, u32[]{:S(2)}, u32[]{:S(2)}) %collective-permute-start.5) | collective-permute-done | bytes 331808 | tf_op jit(solution)/shard_map/ppermute | solution.py:42
  102.5 0.8 add_convert_fusion
  (6 shorter events, 0.1 us)
Async XLA Ops:
  7.2 91.9 %copy-start.1 = (bf16[144,1152]{1,0:T(8,128)(2,1)S(1)}, bf16[144,1152]{1,0:T(8,128)(2,1)}, u32[]{:S(2)}) copy-start(bf16[144,1152]{1,0:T(8,128)(2,1)} %refs_2_.1) | copy-start | bytes 995332
  7.2 80.9 %all-gather.2.cloned.1.call-start = ((), (), s32[]{:S(2)}) async-start(), calls=%async_computation | async-start | bytes 5013504 | tf_op jit(solution)/shard_map/all_gather | solution.py:161
  29.9 20.9 %collective-permute-start = (bf16[144,128]{1,0:T(8,128)(2,1)S(1)}, bf16[144,128]{1,0:T(8,128)(2,1)S(1)}, u32[]{:S(2)}, u32[]{:S(2)}) collective-permute-start(bf16[144,128]{1,0:T(8,128)(2,1)S(1)} %get-tuple-element.18), channel_id=1, source_target_pairs={{0,0},{1,65},{2,130},{3,195},{4,260},{5,325},{6,390},{7,455},{8,8}... | collective-permute-start | bytes 110600 | tf_op jit(solution)/shard_map/ppermute | solution.py:37
  30.6 25.2 %collective-permute-start.1 = (bf16[144,128]{1,0:T(8,128)(2,1)S(1)}, bf16[144,128]{1,0:T(8,128)(2,1)S(1)}, u32[]{:S(2)}, u32[]{:S(2)}) collective-permute-start(bf16[144,128]{1,0:T(8,128)(2,1)S(1)} %get-tuple-element.19), channel_id=1, source_target_pairs={{0,272},{1,337},{2,402},{3,467},{4,20},{5,85},{6,150},{7,215},{8,2... | collective-permute-start | bytes 110600 | tf_op jit(solution)/shard_map/ppermute | solution.py:37
  66.4 9.7 %collective-permute-start.2 = (bf16[8,144,128]{2,1,0:T(8,128)(2,1)S(1)}, bf16[8,144,128]{2,1,0:T(8,128)(2,1)S(1)}, u32[]{:S(2)}, u32[]{:S(2)}) collective-permute-start(bf16[8,144,128]{2,1,0:T(8,128)(2,1)S(1)} %all_gather.6.refs_0_), channel_id=1, source_target_pairs={{0,4},{4,0},{8,12},{12,8},{1,5},{5,1},{9,13},{13,9},{2,6},{6,2},{1... | collective-permute-start | bytes 884744 | tf_op jit(solution)/shard_map/ppermute | solution.py:27
  68.4 11.7 %collective-permute-start.3 = (bf16[8,144,128]{2,1,0:T(8,128)(2,1)S(1)}, bf16[8,144,128]{2,1,0:T(8,128)(2,1)S(1)}, u32[]{:S(2)}, u32[]{:S(2)}) collective-permute-start(bf16[8,144,128]{2,1,0:T(8,128)(2,1)S(1)} %all_gather.6.refs_0_), channel_id=1, source_target_pairs={{0,8},{4,12},{8,0},{12,4},{1,9},{5,13},{9,1},{13,5},{2,10},{6,14},... | collective-permute-start | bytes 884744 | tf_op jit(solution)/shard_map/ppermute | solution.py:27
  70.7 15.1 %collective-permute-start.4 = (bf16[8,144,128]{2,1,0:T(8,128)(2,1)S(1)}, bf16[8,144,128]{2,1,0:T(8,128)(2,1)S(1)}, u32[]{:S(2)}, u32[]{:S(2)}) collective-permute-start(bf16[8,144,128]{2,1,0:T(8,128)(2,1)S(1)} %all_gather.6.refs_0_), channel_id=1, source_target_pairs={{0,12},{4,8},{8,4},{12,0},{1,13},{5,9},{9,5},{13,1},{2,14},{6,10},... | collective-permute-start | bytes 884744 | tf_op jit(solution)/shard_map/ppermute | solution.py:27
  88.0 2.3 %copy-start = (bf16[2048,1152]{1,0:T(8,128)(2,1)S(1)}, bf16[2048,1152]{1,0:T(8,128)(2,1)}, u32[]{:S(2)}) copy-start(bf16[2048,1152]{1,0:T(8,128)(2,1)} %all-gather.2.cloned.1.call-done.refs_1_) | copy-start | bytes 14155780
  91.3 11.2 %collective-permute-start.5 = (bf16[144,1152]{1,0:T(8,128)(2,1)S(1)}, bf16[144,1152]{1,0:T(8,128)(2,1)S(1)}, u32[]{:S(2)}, u32[]{:S(2)}) collective-permute-start(bf16[144,1152]{1,0:T(8,128)(2,1)S(1)} %shard_map.71), channel_id=1, source_target_pairs={{0,32},{16,496},{32,64},{48,16},{64,96},{80,48},{96,128},{112,80},... | collective-permute-start | bytes 995336 | tf_op jit(solution)/shard_map/ppermute | solution.py:42
Sparse Core Ops, SparseCore 0:
  10.1 77.8 all-gather.1

commit v6 on v5

--- a/solution.py
+++ b/solution.py
@@ -72,7 +72,7 @@
         hidden_ref[...], hidden_ref[...], contract, preferred_element_type=jnp.float32
     )
     gram_scaled = jnp.zeros((SEQ, SEQ), jnp.float32)
-    width = 512
+    width = 1152
     for k in range(D // width):
         block = scaled(grad_ref[:, k * width : (k + 1) * width])
         gram_scaled += lax.dot_general(block, block, contract, preferred_element_type=jnp.float32)

time: 111 us -> 112 us (level)
  transfers between devices with their start and end apart: 7 -> 7, of which waited for: 5 -> 4; matrix products, arithmetic and copies ran while one was open for 2% -> 2% of each run, Pallas kernels for 5% -> 5%
where the time goes in v6:
time: 112 us; the launch traced here: 110 us
  starting transfers between devices  36.5 us (33%)
  blocking collectives  29.6 us (26%)
  waiting for transfers between devices  18.6 us (17%)
  between operations  14.2 us (13%)
  Pallas kernels  6.56 us (6%)
  local copies, waits for them, and re-layouts  2.42 us (2%)
  other arithmetic  2.39 us (2%)
    ppermute x2, starting transfers between devices, fan_out(): return lax.ppermute(value, ('pair', 'parity', 'core', 'y', 'x'), perm)  20.7 us
    psum x2, blocking collectives, per_device(): squares = lax.psum(lax.psum(squares, 'x'), 'y')  18.3 us
    all_gather x1, blocking collectives, per_device(): row = lax.all_gather(jnp.stack([keep, swap]), 'x', axis=0, tiled=True)  11.3 us
    ppermute x3, waiting for transfers between devices, along_y(): return lax.ppermute(value, 'y', [(i, i ^ distance) for i in range(ROW)])  10.4 us
    ppermute x3, starting transfers between devices, along_y(): return lax.ppermute(value, 'y', [(i, i ^ distance) for i in range(ROW)])  9.57 us
    ppermute x1, starting transfers between devices, to_neighbour(): return lax.ppermute(value, ('pair', 'parity', 'core'), perm)  6.19 us
    ppermute x2, waiting for transfers between devices, fan_out(): return lax.ppermute(value, ('pair', 'parity', 'core', 'y', 'x'), perm)  5.02 us
    pallas_call x1, Pallas kernels, partial_squares(): pl.pallas_call(squares_kernel, in_specs=[vmem, smem, vmem, vmem], out_spe...  2.82 us
  transfers between devices with their start and end apart: 7, of which 4 were waited for; matrix products, arithmetic and copies ran while one was open for 2% of the time, Pallas kernels for 5%

profile of v6, /device:TPU:1, one launch (start us, length us, event | category | flops | bytes accessed | tf_op | source)
XLA Modules:
  0.0 110.2 jit_solution(6203570727019858279)
XLA Ops:
  7.2 0.0 copy-start.1
  7.2 0.0 all-gather.2.cloned.1.call-start
  7.2 0.7 all-gather.2.cloned.1.call-update
  7.9 2.8 %shard_map.68 = (f32[16,128]{1,0:T(8,128)}, bf16[144,128]{1,0:T(8,128)(2,1)}, bf16[144,128]{1,0:T(8,128)(2,1)}) custom-call(s32[32,128]{1,0:T(8,128)} %bitcast.11, s32[8]{0:T(128)} %count_ref.1, bf16[128,1152]{1,0:T(8,128)(2,1)} %hidden_ref.1, bf16[128,4608]{1,0:T(8,128)(2,1)} %grad_ref.1), custom_call_target="tpu_custom_call" | custom-call | tf_op jit(solution)/shard_map/pallas_call | solution.py:101
  10.7 9.5 %psum.14 = f32[16,128]{1,0:T(8,128)S(1)} all-reduce(f32[16,128]{1,0:T(8,128)} %get-tuple-element.11), channel_id=1, replica_groups=mesh['pair'=8,'parity'=2,'core'=2,'y'=4,'x'=4] {'x'}, use_global_device_ids=true, to_apply=%region_0.0 | all-reduce | flops 2048 | bytes 16384 | tf_op jit(solution)/shard_map/psum | solution.py:166
  20.2 8.8 %psum.15 = f32[16,128]{1,0:T(8,128)S(1)} all-reduce(f32[16,128]{1,0:T(8,128)S(1)} %psum.14), channel_id=1, replica_groups=mesh['pair'=8,'parity'=2,'core'=2,'y'=4,'x'=4] {'y'}, use_global_device_ids=true, to_apply=%region_1.0 | all-reduce | flops 2048 | bytes 16384 | tf_op jit(solution)/shard_map/psum | solution.py:166
  29.1 0.8 multiply_convert_fusion.1
  29.9 0.7 collective-permute-start
  30.6 20.0 %collective-permute-start.1 = (bf16[144,128]{1,0:T(8,128)(2,1)S(1)}, bf16[144,128]{1,0:T(8,128)(2,1)S(1)}, u32[]{:S(2)}, u32[]{:S(2)}) collective-permute-start(bf16[144,128]{1,0:T(8,128)(2,1)S(1)} %get-tuple-element.19), channel_id=1, source_target_pairs={{0,272},{1,337},{2,402},{3,467},{4,20},{5,85},{6,150},{7,215},{8,2... | collective-permute-start | bytes 110600 | tf_op jit(solution)/shard_map/ppermute | solution.py:37
  50.7 0.1 stack_tile.3
  50.8 0.0 collective-permute-done
  50.8 5.0 %collective-permute-done.1 = bf16[144,128]{1,0:T(8,128)(2,1)S(1)} collective-permute-done((bf16[144,128]{1,0:T(8,128)(2,1)S(1)}, bf16[144,128]{1,0:T(8,128)(2,1)S(1)}, u32[]{:S(2)}, u32[]{:S(2)}) %collective-permute-start.1) | collective-permute-done | bytes 36896 | tf_op jit(solution)/shard_map/ppermute | solution.py:37
  55.8 11.3 %all_gather.6.refs_0_ = bf16[8,144,128]{2,1,0:T(8,128)(2,1)S(1)} all-gather(bf16[2,144,128]{2,1,0:T(8,128)(2,1)S(1)} %pad_maximum_fusion), channel_id=1, replica_groups=mesh['pair'=8,'parity'=2,'core'=2,'y'=4,'x'=4] {'x'}, dimensions={0}, use_global_device_ids=true | all-gather | bytes 368640 | tf_op jit(solution)/shard_map/all_gather | solution.py:174
  67.1 1.9 %collective-permute-start.2 = (bf16[8,144,128]{2,1,0:T(8,128)(2,1)S(1)}, bf16[8,144,128]{2,1,0:T(8,128)(2,1)S(1)}, u32[]{:S(2)}, u32[]{:S(2)}) collective-permute-start(bf16[8,144,128]{2,1,0:T(8,128)(2,1)S(1)} %all_gather.6.refs_0_), channel_id=1, source_target_pairs={{0,4},{4,0},{8,12},{12,8},{1,5},{5,1},{9,13},{13,9},{2,6},{6,2},{1... | collective-permute-start | bytes 884744 | tf_op jit(solution)/shard_map/ppermute | solution.py:27
  69.0 1.9 %collective-permute-start.3 = (bf16[8,144,128]{2,1,0:T(8,128)(2,1)S(1)}, bf16[8,144,128]{2,1,0:T(8,128)(2,1)S(1)}, u32[]{:S(2)}, u32[]{:S(2)}) collective-permute-start(bf16[8,144,128]{2,1,0:T(8,128)(2,1)S(1)} %all_gather.6.refs_0_), channel_id=1, source_target_pairs={{0,8},{4,12},{8,0},{12,4},{1,9},{5,13},{9,1},{13,5},{2,10},{6,14},... | collective-permute-start | bytes 884744 | tf_op jit(solution)/shard_map/ppermute | solution.py:27
  70.9 5.7 %collective-permute-start.4 = (bf16[8,144,128]{2,1,0:T(8,128)(2,1)S(1)}, bf16[8,144,128]{2,1,0:T(8,128)(2,1)S(1)}, u32[]{:S(2)}, u32[]{:S(2)}) collective-permute-start(bf16[8,144,128]{2,1,0:T(8,128)(2,1)S(1)} %all_gather.6.refs_0_), channel_id=1, source_target_pairs={{0,12},{4,8},{8,4},{12,0},{1,13},{5,9},{9,5},{13,1},{2,14},{6,10},... | collective-permute-start | bytes 884744 | tf_op jit(solution)/shard_map/ppermute | solution.py:27
  76.7 0.1 add_xor_fusion
  76.8 0.0 collective-permute-done.2.refs_1_
  76.8 4.5 %collective-permute-done.3.refs_2_ = bf16[8,144,128]{2,1,0:T(8,128)(2,1)S(1)} collective-permute-done((bf16[8,144,128]{2,1,0:T(8,128)(2,1)S(1)}, bf16[8,144,128]{2,1,0:T(8,128)(2,1)S(1)}, u32[]{:S(2)}, u32[]{:S(2)}) %collective-permute-start.3) | collective-permute-done | bytes 294944 | tf_op jit(solution)/shard_map/ppermute | solution.py:27
  81.3 5.9 %collective-permute-done.4.refs_3_ = bf16[8,144,128]{2,1,0:T(8,128)(2,1)S(1)} collective-permute-done((bf16[8,144,128]{2,1,0:T(8,128)(2,1)S(1)}, bf16[8,144,128]{2,1,0:T(8,128)(2,1)S(1)}, u32[]{:S(2)}, u32[]{:S(2)}) %collective-permute-start.4) | collective-permute-done | bytes 294944 | tf_op jit(solution)/shard_map/ppermute | solution.py:27
  87.2 1.9 %shard_map.69 = (bf16[144,2048]{1,0:T(8,128)(2,1)S(1)}, bf16[144,2048]{1,0:T(8,128)(2,1)S(1)}) custom-call(s32[2,32]{1,0:T(2,128)S(1)} %pad_add_fusion.place, bf16[8,144,128]{2,1,0:T(8,128)(2,1)S(1)} %all_gather.6.refs_0_, bf16[8,144,128]{2,1,0:T(8,128)(2,1)S(1)} %collective-permute-done.2.refs_1_, bf16[8,144,128]{2,1,0:T(8,128)(2,1)S(1)} %collective-permute-done.3.refs_2_, ...), custom_call_target="tpu_custom_call" | custom-call | tf_op jit(solution)/shard_map/pallas_call | solution.py:124
  89.0 0.0 all-gather.2.cloned.1.call-done.refs_1_
  89.1 0.0 copy-start
  89.1 2.3 %copy-done = bf16[2048,1152]{1,0:T(8,128)(2,1)S(1)} copy-done((bf16[2048,1152]{1,0:T(8,128)(2,1)S(1)}, bf16[2048,1152]{1,0:T(8,128)(2,1)}, u32[]{:S(2)}) %copy-start) | copy-done | bytes 4718616
  91.4 0.9 shard_map.71
  92.3 6.2 %collective-permute-start.5 = (bf16[144,1152]{1,0:T(8,128)(2,1)S(1)}, bf16[144,1152]{1,0:T(8,128)(2,1)S(1)}, u32[]{:S(2)}, u32[]{:S(2)}) collective-permute-start(bf16[144,1152]{1,0:T(8,128)(2,1)S(1)} %shard_map.71), channel_id=1, source_target_pairs={{0,32},{16,496},{32,64},{48,16},{64,96},{80,48},{96,128},{112,80},... | collective-permute-start | bytes 995336 | tf_op jit(solution)/shard_map/ppermute | solution.py:42
  98.5 0.6 fusion.1
  99.2 0.0 copy-done.1
  99.2 0.9 shard_map.70
  100.1 2.5 %collective-permute-done.5 = bf16[144,1152]{1,0:T(8,128)(2,1)S(1)} collective-permute-done((bf16[144,1152]{1,0:T(8,128)(2,1)S(1)}, bf16[144,1152]{1,0:T(8,128)(2,1)S(1)}, u32[]{:S(2)}, u32[]{:S(2)}) %collective-permute-start.5) | collective-permute-done | bytes 331808 | tf_op jit(solution)/shard_map/ppermute | solution.py:42
  102.6 0.8 add_convert_fusion
  (6 shorter events, 0.1 us)
Async XLA Ops:
  7.2 92.0 %copy-start.1 = (bf16[144,1152]{1,0:T(8,128)(2,1)S(1)}, bf16[144,1152]{1,0:T(8,128)(2,1)}, u32[]{:S(2)}) copy-start(bf16[144,1152]{1,0:T(8,128)(2,1)} %refs_2_.1) | copy-start | bytes 995332
  7.2 81.9 %all-gather.2.cloned.1.call-start = ((), (), s32[]{:S(2)}) async-start(), calls=%async_computation | async-start | bytes 5013504 | tf_op jit(solution)/shard_map/all_gather | solution.py:161
  29.9 20.9 %collective-permute-start = (bf16[144,128]{1,0:T(8,128)(2,1)S(1)}, bf16[144,128]{1,0:T(8,128)(2,1)S(1)}, u32[]{:S(2)}, u32[]{:S(2)}) collective-permute-start(bf16[144,128]{1,0:T(8,128)(2,1)S(1)} %get-tuple-element.18), channel_id=1, source_target_pairs={{0,0},{1,65},{2,130},{3,195},{4,260},{5,325},{6,390},{7,455},{8,8}... | collective-permute-start | bytes 110600 | tf_op jit(solution)/shard_map/ppermute | solution.py:37
  30.6 25.2 %collective-permute-start.1 = (bf16[144,128]{1,0:T(8,128)(2,1)S(1)}, bf16[144,128]{1,0:T(8,128)(2,1)S(1)}, u32[]{:S(2)}, u32[]{:S(2)}) collective-permute-start(bf16[144,128]{1,0:T(8,128)(2,1)S(1)} %get-tuple-element.19), channel_id=1, source_target_pairs={{0,272},{1,337},{2,402},{3,467},{4,20},{5,85},{6,150},{7,215},{8,2... | collective-permute-start | bytes 110600 | tf_op jit(solution)/shard_map/ppermute | solution.py:37
  67.1 9.7 %collective-permute-start.2 = (bf16[8,144,128]{2,1,0:T(8,128)(2,1)S(1)}, bf16[8,144,128]{2,1,0:T(8,128)(2,1)S(1)}, u32[]{:S(2)}, u32[]{:S(2)}) collective-permute-start(bf16[8,144,128]{2,1,0:T(8,128)(2,1)S(1)} %all_gather.6.refs_0_), channel_id=1, source_target_pairs={{0,4},{4,0},{8,12},{12,8},{1,5},{5,1},{9,13},{13,9},{2,6},{6,2},{1... | collective-permute-start | bytes 884744 | tf_op jit(solution)/shard_map/ppermute | solution.py:27
  69.0 12.3 %collective-permute-start.3 = (bf16[8,144,128]{2,1,0:T(8,128)(2,1)S(1)}, bf16[8,144,128]{2,1,0:T(8,128)(2,1)S(1)}, u32[]{:S(2)}, u32[]{:S(2)}) collective-permute-start(bf16[8,144,128]{2,1,0:T(8,128)(2,1)S(1)} %all_gather.6.refs_0_), channel_id=1, source_target_pairs={{0,8},{4,12},{8,0},{12,4},{1,9},{5,13},{9,1},{13,5},{2,10},{6,14},... | collective-permute-start | bytes 884744 | tf_op jit(solution)/shard_map/ppermute | solution.py:27
  70.9 16.2 %collective-permute-start.4 = (bf16[8,144,128]{2,1,0:T(8,128)(2,1)S(1)}, bf16[8,144,128]{2,1,0:T(8,128)(2,1)S(1)}, u32[]{:S(2)}, u32[]{:S(2)}) collective-permute-start(bf16[8,144,128]{2,1,0:T(8,128)(2,1)S(1)} %all_gather.6.refs_0_), channel_id=1, source_target_pairs={{0,12},{4,8},{8,4},{12,0},{1,13},{5,9},{9,5},{13,1},{2,14},{6,10},... | collective-permute-start | bytes 884744 | tf_op jit(solution)/shard_map/ppermute | solution.py:27
  89.1 2.3 %copy-start = (bf16[2048,1152]{1,0:T(8,128)(2,1)S(1)}, bf16[2048,1152]{1,0:T(8,128)(2,1)}, u32[]{:S(2)}) copy-start(bf16[2048,1152]{1,0:T(8,128)(2,1)} %all-gather.2.cloned.1.call-done.refs_1_) | copy-start | bytes 14155780
  92.3 10.2 %collective-permute-start.5 = (bf16[144,1152]{1,0:T(8,128)(2,1)S(1)}, bf16[144,1152]{1,0:T(8,128)(2,1)S(1)}, u32[]{:S(2)}, u32[]{:S(2)}) collective-permute-start(bf16[144,1152]{1,0:T(8,128)(2,1)S(1)} %shard_map.71), channel_id=1, source_target_pairs={{0,32},{16,496},{32,64},{48,16},{64,96},{80,48},{96,128},{112,80},... | collective-permute-start | bytes 995336 | tf_op jit(solution)/shard_map/ppermute | solution.py:42
Sparse Core Ops, SparseCore 0:
  10.1 77.4 all-gather.1
